TPU v7x, 32 devices: a whole 2x2x4 slice. The times are simulated.
32 devices in a mesh: dp: 16 (over z, x, core), tensor: 2 (over y).
Axes of the slice: x: 2, y: 2, z: 4, core: 2. Of those that a mesh axis runs over, the one named last changes fastest.
Arguments:
- tokens: bfloat16 [512, 64, 768], P('tensor', 'dp'), may hold values from -6 to 6
- lengths: int32 [64], P('dp'), may hold values from 64 to 512, as said below
- w_qkv: bfloat16 [3, 768, 768], P(None, 'dp', 'tensor'), may hold values from -0.21875 to 0.21875
- qkv_bias: bfloat16 [2, 768], P(None, ('tensor', 'dp')), may hold values from -3 to 3
- w_out: bfloat16 [768, 768], P('tensor', 'dp'), may hold values from -0.875 to 0.875
- w_in: bfloat16 [768, 3072], P('dp', 'tensor'), may hold values from -0.21875 to 0.21875
- b_in: bfloat16 [3072], P(('tensor', 'dp')), may hold values from -3 to 3
- w_down: bfloat16 [3072, 768], P('tensor', 'dp'), may hold values from -0.109375 to 0.109375
- norm_gains: bfloat16 [2, 768], P(None, ('tensor', 'dp')), may hold values from 0.5 to 1.5
- row_biases: bfloat16 [4, 768], P(None, ('tensor', 'dp')), may hold values from -2 to 2
- cotangent: bfloat16 [512, 64, 768], P('tensor', 'dp'), may hold values from -6 to 6
Outputs:
- out: bfloat16 [512, 64, 768], P('tensor', 'dp')
- d_tokens: float32 [512, 64, 768], P('tensor', 'dp')
- grad_qkv: float32 [3, 768, 768], P(None, 'dp', 'tensor')
- grad_qkv_bias: float32 [2, 768], P(None, ('tensor', 'dp'))
- grad_out: float32 [768, 768], P('tensor', 'dp')
- grad_in: float32 [768, 3072], P('dp', 'tensor')
- grad_in_bias: float32 [3072], P(('tensor', 'dp'))
- grad_down: float32 [3072, 768], P('tensor', 'dp')
- grad_gains: float32 [2, 768], P(None, ('tensor', 'dp'))
- grad_biases: float32 [4, 768], P(None, ('tensor', 'dp'))
Inputs may be any that keep to these rules, and one draw needn't show every extreme that they name: `lengths`: each aligned run of 4 sequences holds at least one sequence of length 512; which one is drawn.
All inputs are finite; a program needn't handle non-finite values.
Results may differ from a plain program's by a relative error of at most 0.017.
Values may be sent and summed in bfloat16 or wider, within the bound.
No kernel may reach another device: no remote copies, remote signals or barrier semaphores. Data moves between devices by JAX's collectives and lax.ppermute only.
A program may use at most 192 MiB of HBM per device.

v0:
```python
import math

import jax
import jax.numpy as jnp
from jax import lax
from jax.sharding import PartitionSpec as P

HEAD_DIM = 64


norm_eps = 1e-12


def norm_forward(values, gain, shift):
    centered = values - jnp.mean(values, axis=-1, keepdims=True)
    inverse = lax.rsqrt(jnp.mean(centered * centered, axis=-1, keepdims=True) + norm_eps)
    normed = centered * inverse
    return (normed * gain + shift, normed, inverse)


def norm_backward(grad, normed, inverse, gain):
    scaled = grad * gain
    inner = (
        scaled
        - jnp.mean(scaled, axis=-1, keepdims=True)
        - normed * jnp.mean(scaled * normed, axis=-1, keepdims=True)
    )
    return inner * inverse


def masked_scores(query, keys, length):
    scale_factor = 1.0 / math.sqrt(HEAD_DIM)
    scores = (
        jnp.einsum("lhe,mhe->hlm", query, keys, preferred_element_type=jnp.float32) * scale_factor
    )
    valid = jnp.arange(query.shape[0], dtype=jnp.int32) < length
    return jnp.where(valid[None, None, :], scores, -1000000000.0)


def attend(query, keys, values, length):
    scores = masked_scores(query, keys, length)
    peak = jnp.max(scores, axis=-1, keepdims=True)
    exponent = jnp.exp(scores - peak)
    total = jnp.sum(exponent, axis=-1, keepdims=True)
    probs = (exponent / total).astype(jnp.bfloat16)
    context = jnp.einsum("hlm,mhe->lhe", probs, values, preferred_element_type=jnp.float32)
    return (context.astype(jnp.bfloat16), (peak + jnp.log(total))[..., 0])


def attend_back(query, keys, values, length, logsum, grad_ctx):
    scale_factor = 1.0 / math.sqrt(HEAD_DIM)
    probs = jnp.exp(masked_scores(query, keys, length) - logsum[..., None])
    grad_probs = jnp.einsum("lhe,mhe->hlm", grad_ctx, values, preferred_element_type=jnp.float32)
    grad_values = jnp.einsum(
        "hlm,lhe->mhe", probs.astype(jnp.bfloat16), grad_ctx, preferred_element_type=jnp.float32
    )
    grad_scores = (
        probs * (grad_probs - jnp.sum(grad_probs * probs, axis=-1, keepdims=True))
    ).astype(jnp.bfloat16)
    grad_query = (
        jnp.einsum("hlm,mhe->lhe", grad_scores, keys, preferred_element_type=jnp.float32)
        * scale_factor
    )
    grad_keys = (
        jnp.einsum("hlm,lhe->mhe", grad_scores, query, preferred_element_type=jnp.float32)
        * scale_factor
    )
    return (
        grad_query.astype(jnp.bfloat16),
        grad_keys.astype(jnp.bfloat16),
        grad_values.astype(jnp.bfloat16),
    )


def shards(
    tokens, lengths, w_qkv, qkv_bias, w_out, w_in, b_in, w_down, norm_gains, row_biases, cotangent
):
    half_len, seq_count, width = tokens.shape
    proj_all, bias_pair, out_rows, gain_half, shift_half = (
        lax.all_gather(w_qkv, "dp", axis=1, tiled=True),
        lax.all_gather(qkv_bias, "dp", axis=1, tiled=True),
        lax.all_gather(w_out, "dp", axis=1, tiled=True),
        lax.all_gather(norm_gains, "dp", axis=1, tiled=True),
        lax.all_gather(row_biases, "dp", axis=1, tiled=True),
    )
    whole_in, gains_low, shifts_low = (
        lax.all_gather(tokens, "tensor", axis=0, tiled=True),
        lax.all_gather(gain_half, "tensor", axis=1, tiled=True),
        lax.all_gather(shift_half, "tensor", axis=1, tiled=True),
    )
    gains = gains_low.astype(jnp.float32)
    shifts = shifts_low.astype(jnp.float32)
    seq_len = whole_in.shape[0]
    local_width = proj_all.shape[2]
    local_heads = local_width // HEAD_DIM
    own_rows = half_len * seq_count
    rows = whole_in.reshape(seq_len * seq_count, width)

    def by_sequence(matrix):
        return jnp.moveaxis(matrix.reshape(seq_len, seq_count, local_heads, HEAD_DIM), 1, 0)

    def to_rows(matrix):
        return jnp.moveaxis(matrix, 0, 1).reshape(seq_len * seq_count, local_width)

    projected = jnp.einsum("td,cde->cte", rows, proj_all, preferred_element_type=jnp.float32)
    query = (projected[0] + bias_pair[0]).astype(jnp.bfloat16)
    keys = projected[1].astype(jnp.bfloat16)
    values = (projected[2] + bias_pair[1]).astype(jnp.bfloat16)
    seq_query, seq_keys, seq_values = (by_sequence(query), by_sequence(keys), by_sequence(values))
    context, logsum = lax.map(
        lambda item: attend(item[0], item[1], item[2], item[3]),
        (seq_query, seq_keys, seq_values, lengths),
    )
    ctx_rows = to_rows(context)
    attended = lax.psum_scatter(
        jnp.dot(ctx_rows, out_rows, preferred_element_type=jnp.float32).astype(jnp.bfloat16),
        "tensor",
        scatter_dimension=0,
        tiled=True,
    ).astype(jnp.float32)
    own_input = tokens.astype(jnp.float32).reshape(own_rows, width)
    first, normed_one, inverse_one = norm_forward(
        own_input + attended + shifts[0], gains[0], shifts[1]
    )
    first_low = first.astype(jnp.bfloat16).reshape(half_len, seq_count, width)
    first_all = lax.all_gather(first_low, "tensor", axis=0, tiled=True).reshape(
        seq_len * seq_count, width
    )
    w_in_all, b_in_all, w_down_all = (
        lax.all_gather(w_in, "dp", axis=0, tiled=True),
        lax.all_gather(b_in, "dp", axis=0, tiled=True),
        lax.all_gather(w_down, "dp", axis=1, tiled=True),
    )
    before = jnp.dot(first_all, w_in_all, preferred_element_type=jnp.float32) + b_in_all
    hidden = jax.nn.gelu(before, approximate=False).astype(jnp.bfloat16)
    mixed = lax.psum_scatter(
        jnp.dot(hidden, w_down_all, preferred_element_type=jnp.float32).astype(jnp.bfloat16),
        "tensor",
        scatter_dimension=0,
        tiled=True,
    ).astype(jnp.float32)
    output, normed_two, inverse_two = norm_forward(first + mixed + shifts[2], gains[1], shifts[3])
    out = output.astype(jnp.bfloat16).reshape(tokens.shape)
    grad_output = cotangent.astype(jnp.float32).reshape(own_rows, width)
    grad_gain_two = jnp.sum(grad_output * normed_two, axis=0)
    grad_shift_two = jnp.sum(grad_output, axis=0)
    grad_second = norm_backward(grad_output, normed_two, inverse_two, gains[1])
    grad_down_bias = jnp.sum(grad_second, axis=0)
    mixed_grad = lax.all_gather(
        grad_second.astype(jnp.bfloat16).reshape(half_len, seq_count, width),
        "tensor",
        axis=0,
        tiled=True,
    ).reshape(seq_len * seq_count, width)
    w_in_all, w_down_all = (
        lax.all_gather(w_in, "dp", axis=0, tiled=True),
        lax.all_gather(w_down, "dp", axis=1, tiled=True),
    )
    grad_w_down = jnp.einsum("tf,td->fd", hidden, mixed_grad, preferred_element_type=jnp.float32)
    grad_hidden = jnp.einsum(
        "td,fd->tf", mixed_grad, w_down_all, preferred_element_type=jnp.float32
    )
    gelu_pull = jax.vjp(lambda value: jax.nn.gelu(value, approximate=False), before)[1]
    grad_before = gelu_pull(grad_hidden)[0].astype(jnp.bfloat16)
    grad_in_bias = jnp.sum(grad_before, axis=0, dtype=jnp.float32)
    grad_w_in = jnp.einsum("td,tf->df", first_all, grad_before, preferred_element_type=jnp.float32)
    grad_first = (
        lax.psum_scatter(
            jnp.einsum(
                "tf,df->td", grad_before, w_in_all, preferred_element_type=jnp.float32
            ).astype(jnp.bfloat16),
            "tensor",
            scatter_dimension=0,
            tiled=True,
        ).astype(jnp.float32)
        + grad_second
    )
    mlp_grads = (
        lax.psum_scatter(grad_w_in, "dp", scatter_dimension=0, tiled=True),
        lax.psum_scatter(grad_in_bias, "dp", scatter_dimension=0, tiled=True),
        lax.psum_scatter(grad_w_down, "dp", scatter_dimension=1, tiled=True),
    )
    grad_gain_one = jnp.sum(grad_first * normed_one, axis=0)
    grad_shift_one = jnp.sum(grad_first, axis=0)
    grad_resid = norm_backward(grad_first, normed_one, inverse_one, gains[0])
    grad_out_bias = jnp.sum(grad_resid, axis=0)
    attn_grad = lax.all_gather(
        grad_resid.astype(jnp.bfloat16).reshape(half_len, seq_count, width),
        "tensor",
        axis=0,
        tiled=True,
    ).reshape(seq_len * seq_count, width)
    proj_all, out_rows = (
        lax.all_gather(w_qkv, "dp", axis=1, tiled=True),
        lax.all_gather(w_out, "dp", axis=1, tiled=True),
    )
    grad_w_out = jnp.einsum("te,td->ed", ctx_rows, attn_grad, preferred_element_type=jnp.float32)
    grad_ctx = jnp.einsum(
        "td,ed->te", attn_grad, out_rows, preferred_element_type=jnp.float32
    ).astype(jnp.bfloat16)
    grad_query, grad_keys, grad_values = lax.map(
        lambda item: attend_back(item[0], item[1], item[2], item[3], item[4], item[5]),
        (seq_query, seq_keys, seq_values, lengths, logsum, by_sequence(grad_ctx)),
    )
    grad_stack = jnp.stack([to_rows(grad_query), to_rows(grad_keys), to_rows(grad_values)])
    grad_pair = jnp.stack(
        [
            jnp.sum(grad_stack[0], axis=0, dtype=jnp.float32),
            jnp.sum(grad_stack[2], axis=0, dtype=jnp.float32),
        ]
    )
    grad_proj = jnp.einsum("td,cte->cde", rows, grad_stack, preferred_element_type=jnp.float32)
    grad_rows = jnp.einsum("cte,cde->td", grad_stack, proj_all, preferred_element_type=jnp.float32)
    gain_part = jnp.stack([grad_gain_one, grad_gain_two])
    shift_part = jnp.stack([grad_out_bias, grad_shift_one, grad_down_bias, grad_shift_two])
    grad_inputs, gain_sum, shift_sum = (
        lax.psum_scatter(
            grad_rows.reshape(seq_len, seq_count, width).astype(jnp.bfloat16),
            "tensor",
            scatter_dimension=0,
            tiled=True,
        ).astype(jnp.float32),
        lax.psum_scatter(
            gain_part.astype(jnp.bfloat16), "tensor", scatter_dimension=1, tiled=True
        ).astype(jnp.float32),
        lax.psum_scatter(
            shift_part.astype(jnp.bfloat16), "tensor", scatter_dimension=1, tiled=True
        ).astype(jnp.float32),
    )
    d_tokens = grad_inputs + grad_resid.reshape(tokens.shape)
    attn_grads = (
        lax.psum_scatter(grad_proj, "dp", scatter_dimension=1, tiled=True),
        lax.psum_scatter(grad_pair, "dp", scatter_dimension=1, tiled=True),
        lax.psum_scatter(grad_w_out, "dp", scatter_dimension=1, tiled=True),
        lax.psum_scatter(gain_sum, "dp", scatter_dimension=1, tiled=True),
        lax.psum_scatter(shift_sum, "dp", scatter_dimension=1, tiled=True),
    )
    return (
        out,
        d_tokens,
        attn_grads[0],
        attn_grads[1],
        attn_grads[2],
        mlp_grads[0],
        mlp_grads[1],
        mlp_grads[2],
        attn_grads[3],
        attn_grads[4],
    )


def solution(mesh):
    placed = (
        P("tensor", "dp", None),
        P("dp"),
        P(None, "dp", "tensor"),
        P(None, ("tensor", "dp")),
        P("tensor", "dp"),
        P("dp", "tensor"),
        P(("tensor", "dp")),
        P("tensor", "dp"),
        P(None, ("tensor", "dp")),
        P(None, ("tensor", "dp")),
        P("tensor", "dp", None),
    )
    return jax.shard_map(
        shards,
        mesh=mesh,
        in_specs=placed,
        out_specs=(
            P("tensor", "dp", None),
            P("tensor", "dp", None),
            P(None, "dp", "tensor"),
            P(None, ("tensor", "dp")),
            P("tensor", "dp"),
            P("dp", "tensor"),
            P(("tensor", "dp")),
            P("tensor", "dp"),
            P(None, ("tensor", "dp")),
            P(None, ("tensor", "dp")),
        ),
        check_vma=False,
    )
```

profile of v0, /device:TPU:0, one launch (start us, length us, event | category | flops | bytes accessed | tf_op | source)
XLA Modules:
  0.0 1208.4 jit_solution(1625613009765085751)
XLA Ops:
  8.7 23.1 %all-gather = bf16[16,24,2]{1,2,0:T(2,128)(2,1)S(1)} all-gather(bf16[1,24,2]{1,2,0:T(2,128)(2,1)} %bitcast.192), channel_id=1, replica_groups=mesh['dp'=16,'tensor'=2] {'dp'}, dimensions={0}, use_global_device_ids=true | all-gather | bytes 1632 | tf_op jit(solution)/shard_map/all_gather | solution.py:81
  32.1 20.6 %all_gather.49 = bf16[384,768]{0,1:T(8,128)(2,1)} all-gather(bf16[384,48]{0,1:T(8,128)(2,1)} %param.19), channel_id=1, replica_groups=mesh['dp'=16,'tensor'=2] {'dp'}, dimensions={1}, use_global_device_ids=true | all-gather | bytes 626688 | tf_op jit(solution)/shard_map/all_gather | solution.py:82
  61.8 38.2 %all-gather.11.cloned.1.call-done = bf16[3,768,384]{2,1,0:T(8,128)(2,1)} async-done(((bf16[3,48,384]{2,1,0:T(8,128)(2,1)}), bf16[3,768,384]{2,1,0:T(8,128)(2,1)}) %all-gather.11.cloned.1.call-update) | async-done | bytes 1769488 | tf_op jit(solution)/shard_map/all_gather | solution.py:80
  100.0 5.4 convolution_bitcast_fusion
  112.4 6.6 squeeze.41
  119.0 6.4 fusion.65
  125.4 5.1 copy.65
  132.9 6.6 squeeze.42
  139.5 6.4 fusion.66
  151.7 5.9 convert_element_type.132
  163.1 33.4 %while.26 = (s32[]{:T(128)}, bf16[4,512,6,64]{1,3,2,0:T(8,128)(2,1)}, f32[4,6,512]{2,1,0:T(8,128)}, bf16[4,512,6,64]{1,3,2,0:T(8,128)(2,1)}, s32[4]{0:T(128)S(1)...) while((s32[]{:T(128)}, bf16[4,512,6,64]{1,3,2,0:T(8,128)(2,1)}, ...), condition=%wide.region_3.4_spmd, body=%wide.region_0.3_spmd.sunk | while | flops 421721600 | bytes 20554340 | solution.py:110
  196.5 7.7 copy.68
  204.2 6.1 reshape.176
  210.3 5.0 convolution_convert_fusion
  218.5 19.3 %all-gather.1 = bf16[16,24,4]{1,2,0:T(4,128)(2,1)S(1)} all-gather(bf16[1,24,4]{1,2,0:T(4,128)(2,1)S(1)} %bitcast.191), channel_id=1, replica_groups=mesh['dp'=16,'tensor'=2] {'dp'}, dimensions={0}, use_global_device_ids=true | all-gather | bytes 3264 | tf_op jit(solution)/shard_map/all_gather | solution.py:84
  242.3 17.0 %all-gather.2 = bf16[16,24,2]{1,2,0:T(2,128)(2,1)S(1)} all-gather(bf16[1,24,2]{1,2,0:T(2,128)(2,1)S(1)} %bitcast.193), channel_id=1, replica_groups=mesh['dp'=16,'tensor'=2] {'dp'}, dimensions={0}, use_global_device_ids=true | all-gather | bytes 1632 | tf_op jit(solution)/shard_map/all_gather | solution.py:83
  275.6 30.2 %all-reduce = bf16[1536]{0:T(1024)(128)(2,1)S(1)} all-reduce(bf16[1536]{0:T(1024)(128)(2,1)S(1)} %dynamic-update-slice), channel_id=1, replica_groups=mesh['dp'=16,'tensor'=2] {'dp'}, use_global_device_ids=true, to_apply=%add | all-reduce | flops 1536 | bytes 6144
  305.8 10.8 all-gather.15.cloned.1.call-done
  316.6 16.6 %reshape.178 = bf16[2048,768]{1,0:T(8,128)(2,1)} reshape(bf16[512,4,768]{2,1,0:T(4,128)(2,1)} %all-gather.15.cloned.1.call-done) | data formatting | bytes 6291456 | tf_op jit(solution)/shard_map/reshape | solution.py:126
  333.2 28.1 %all-gather.17.cloned.1.call-done = bf16[768,1536]{1,0:T(8,128)(2,1)} async-done(((bf16[48,1536]{1,0:T(8,128)(2,1)}), bf16[768,1536]{1,0:T(8,128)(2,1)}) %all-gather.17.cloned.1.call-update) | async-done | bytes 2359312 | tf_op jit(solution)/shard_map/all_gather | solution.py:130
  361.3 34.9 %multiply_convert_fusion.1 = (bf16[2048,1536]{1,0:T(8,128)(2,1)}, f32[2048,1536]{1,0:T(8,128)}, f32[2048,1536]{1,0:T(8,128)}) fusion(f32[1536]{0:T(1024)S(1)} %convert_element_type.138, bf16[2048,768]{1,0:T(8,128)(2,1)} %reshape.178, bf16[768,1536]{1,0:T(8,128)(2,1)} %all-gather.17.cloned.1.call-done), kind=kOutput, calls=%fused_computation.68 | convolution fusion | flops 5039456256 | bytes 36968448 | tf_op jit(solution)/shard_map/dot_general | solution.py:134
  396.2 8.7 all-gather.19.cloned.1.call-done
  404.9 9.0 convolution_convert_fusion.2
  420.9 35.4 %reduce-scatter.18.cloned.1.call-done = bf16[1024,768]{1,0:T(8,128)(2,1)} async-done(((bf16[2048,768]{1,0:T(8,128)(2,1)}), bf16[1024,768]{1,0:T(8,128)(2,1)}) %reduce-scatter.18.cloned.1.call-update) | async-done | bytes 1572880 | tf_op jit(solution)/shard_map/reduce_scatter | solution.py:136
  469.3 45.0 %all-gather.21.cloned.1.call-done = bf16[512,4,768]{2,1,0:T(4,128)(2,1)} async-done(((bf16[256,4,768]{2,1,0:T(4,128)(2,1)}), bf16[512,4,768]{2,1,0:T(4,128)(2,1)}) %all-gather.21.cloned.1.call-update) | async-done | bytes 3145744 | tf_op jit(solution)/shard_map/all_gather | solution.py:149
  514.3 6.4 reshape.182
  520.7 17.6 %convert_reduce_fusion = (f32[1536]{0:T(1024)}, bf16[2048,1536]{1,0:T(8,128)(2,1)S(1)}) fusion(f32[2048,1536]{1,0:T(8,128)} %get-tuple-element.231, bf16[2048,768]{1,0:T(8,128)(2,1)} %reshape.182, bf16[1536,768]{0,1:T(8,128)(2,1)} %all-gather.19.cloned.1.call-done, f32[2048,1536]{1,0:T(8,128)} %get-tuple-element.243, f32[1536]{0:T(1024)S(1)} %convert_element_type.138), kind=kOutput, calls=%fused_computation.66 | convolution fusion | flops 4885314048 | bytes 36974592 | tf_op jit(solution)/shard_map/td,fd->tf/dot_general | solution.py:160
  540.9 6.5 convolution_convert_fusion.1
  547.5 43.5 %reduce-scatter.20.cloned.1.call-done = bf16[1024,768]{1,0:T(8,128)(2,1)} async-done(((bf16[2048,768]{1,0:T(8,128)(2,1)}), bf16[1024,768]{1,0:T(8,128)(2,1)}) %reduce-scatter.20.cloned.1.call-update) | async-done | bytes 1572880 | tf_op jit(solution)/shard_map/reduce_scatter | solution.py:168
  602.5 41.9 %all-gather.23.cloned.1.call-done = bf16[512,4,768]{2,1,0:T(4,128)(2,1)} async-done(((bf16[256,4,768]{2,1,0:T(4,128)(2,1)}), bf16[512,4,768]{2,1,0:T(4,128)(2,1)}) %all-gather.23.cloned.1.call-update) | async-done | bytes 3145744 | tf_op jit(solution)/shard_map/all_gather | solution.py:187
  653.5 5.9 reshape.185
  659.4 5.1 copy.73
  668.5 55.8 %while.27 = (s32[]{:T(128)}, bf16[4,512,6,64]{1,3,2,0:T(8,128)(2,1)}, bf16[4,512,6,64]{1,3,2,0:T(8,128)(2,1)}, bf16[4,512,6,64]{1,3,2,0:T(8,128)(2,1)}, bf16[4,5...) while((s32[]{:T(128)}, ...), condition=%wide.region_17.18_spmd, body=%wide.region_15.17_spmd.sunk | while | flops 1031206400 | bytes 57511068 | solution.py:201
  724.2 7.4 copy.75
  731.6 5.5 stack_reshape.9
  738.5 6.7 copy.76
  745.1 5.2 stack_reshape.10
  750.3 7.4 copy.77
  757.7 5.2 stack_reshape.11
  765.6 6.3 convolution_bitcast_fusion.1
  776.2 7.2 bitcast_convert_fusion
  787.8 9.6 fusion.80
  799.3 9.6 fusion.79
  830.4 62.1 %all-reduce.7 = (f32[2,384]{1,0:T(2,128)S(1)}, f32[1536]{0:T(1024)S(1)}, f32[2,384]{1,0:T(2,128)S(1)}, f32[4,384]{1,0:T(4,128)S(1)}) all-reduce(f32[2,384]{1,0:T(2,128)S(1)} %pad_maximum_fusion.1, f32[1536]{0:T(1024)S(1)} %copy-done.21, bf16[2,384]{1,0:T(2,128)(2,1)S(1)} %copy.89, ...), channel_id=7, replica_groups=mesh['dp'=16,'tensor'=2] {'dp'}, use_global_device_ids=true, to_apply=%region_22.23.clone | all-reduce | flops 4608 | bytes 32256
  896.7 84.3 %all-reduce.11.cloned.1.call-done = bf16[512,4,768]{2,1,0:T(4,128)(2,1)} async-done(((bf16[512,4,768]{2,1,0:T(4,128)(2,1)}), bf16[512,4,768]{2,1,0:T(4,128)(2,1)}) %all-reduce.11.cloned.1.call-update) | async-done | bytes 3145744
  984.9 76.0 %reduce-scatter.26.cloned.1.call-done = f32[1536,48]{0,1:T(8,128)} async-done(((f32[1536,768]{0,1:T(8,128)}), f32[1536,48]{0,1:T(8,128)}) %reduce-scatter.26.cloned.1.call-update) | async-done | bytes 294928 | tf_op jit(solution)/shard_map/reduce_scatter | solution.py:181
  1060.9 79.5 %reduce-scatter.24.cloned.1.call-done = f32[48,1536]{1,0:T(8,128)} async-done(((f32[768,1536]{1,0:T(8,128)}), f32[48,1536]{1,0:T(8,128)}) %reduce-scatter.24.cloned.1.call-update) | async-done | bytes 294928 | tf_op jit(solution)/shard_map/reduce_scatter | solution.py:179
  1140.4 61.1 %reduce-scatter.22.cloned.1.call-done = f32[384,48]{0,1:T(8,128)} async-done(((f32[384,768]{0,1:T(8,128)}), f32[384,48]{0,1:T(8,128)}) %reduce-scatter.22.cloned.1.call-update) | async-done | bytes 73744 | tf_op jit(solution)/shard_map/reduce_scatter | solution.py:234
  (259 shorter events, 231.7 us)
Async XLA Ops:
  7.2 50.0 %all-gather.13.cloned.1.call-start = ((), (), s32[]{:S(2)}) async-start(), calls=%async_computation.9 | async-start | bytes 4718592 | tf_op jit(solution)/shard_map/all_gather | solution.py:87
  7.9 92.1 %all-gather.11.cloned.1.call-start = ((), (), s32[]{:S(2)}) async-start(), calls=%async_computation.8 | async-start | bytes 1880064 | tf_op jit(solution)/shard_map/all_gather | solution.py:80
  8.7 255.2 %reduce-scatter.16.cloned.1.call-start = ((), (), s32[]{:S(2)}) async-start(), calls=%async_computation.10 | async-start | bytes 4718592 | tf_op jit(solution)/shard_map/reduce_scatter | solution.py:115
  61.7 38.2 %copy-start.15 = (bf16[2048,768,1]{1,0,2:T(8,128)(2,1)}, bf16[2048,768,1]{1,0,2:T(8,128)(2,1)S(1)}, u32[]{:S(2)}) copy-start(bf16[2048,768,1]{1,0,2:T(8,128)(2,1)S(1)} %reshape.202) | copy-start | bytes 9437188
  145.9 4.3 copy-start.11
  157.6 5.5 copy-start.27
  196.5 13.8 %copy-start = (bf16[4,512,6,64]{1,3,2,0:T(8,128)(2,1)}, bf16[4,512,6,64]{1,3,2,0:T(8,128)(2,1)S(1)}, u32[]{:S(2)}) copy-start(bf16[4,512,6,64]{1,3,2,0:T(8,128)(2,1)S(1)} %get-tuple-element.434) | copy-start | bytes 4718596
  196.5 13.8 %copy-start.2 = (bf16[4,512,6,64]{1,3,2,0:T(8,128)(2,1)}, bf16[4,512,6,64]{1,3,2,0:T(8,128)(2,1)S(1)}, u32[]{:S(2)}) copy-start(bf16[4,512,6,64]{1,3,2,0:T(8,128)(2,1)S(1)} %get-tuple-element.435) | copy-start | bytes 4718596
  215.3 3.1 copy-start.23
  215.3 26.9 %copy-start.24 = (bf16[2,24]{1,0:T(2,128)(2,1)S(1)}, bf16[2,24]{1,0:T(2,128)(2,1)}, u32[]{:S(2)}) copy-start(bf16[2,24]{1,0:T(2,128)(2,1)} %param.23) | copy-start | bytes 292
  215.4 101.3 %all-gather.15.cloned.1.call-start = ((), (), s32[]{:S(2)}) async-start(), calls=%async_computation.11 | async-start | bytes 4718592 | tf_op jit(solution)/shard_map/all_gather | solution.py:126
  268.9 5.2 copy-start.22
  268.9 6.4 copy-start.26
  272.9 88.5 %all-gather.17.cloned.1.call-start = ((), (), s32[]{:S(2)}) async-start(), calls=%async_computation.12 | async-start | bytes 2506752 | tf_op jit(solution)/shard_map/all_gather | solution.py:130
  273.4 131.4 %all-gather.19.cloned.1.call-start = ((), (), s32[]{:S(2)}) async-start(), calls=%async_computation.13 | async-start | bytes 2506752 | tf_op jit(solution)/shard_map/all_gather | solution.py:132
  274.0 182.2 %reduce-scatter.18.cloned.1.call-start = ((), (), s32[]{:S(2)}) async-start(), calls=%async_computation.14 | async-start | bytes 4718592 | tf_op jit(solution)/shard_map/reduce_scatter | solution.py:136
  414.0 100.4 %all-gather.21.cloned.1.call-start = ((), (), s32[]{:S(2)}) async-start(), calls=%async_computation.15 | async-start | bytes 4718592 | tf_op jit(solution)/shard_map/all_gather | solution.py:149
  469.2 121.7 %reduce-scatter.20.cloned.1.call-start = ((), (), s32[]{:S(2)}) async-start(), calls=%async_computation.16 | async-start | bytes 4718592 | tf_op jit(solution)/shard_map/reduce_scatter | solution.py:168
  520.7 20.2 %copy-start.25 = (bf16[768,1536]{1,0:T(8,128)(2,1)S(1)}, bf16[768,1536]{1,0:T(8,128)(2,1)}, u32[]{:S(2)}) copy-start(bf16[768,1536]{1,0:T(8,128)(2,1)} %all-gather.17.cloned.1.call-done) | copy-start | bytes 7077892
  538.2 2.7 copy-start.30
  547.4 97.0 %all-gather.23.cloned.1.call-start = ((), (), s32[]{:S(2)}) async-start(), calls=%async_computation.17 | async-start | bytes 4718592 | tf_op jit(solution)/shard_map/all_gather | solution.py:187
  590.9 3.6 copy-start.6
  590.9 3.8 copy-start.14
  597.9 2.0 copy-start.8
  599.3 225.4 %reduce-scatter.28.cloned.1.call-start = ((), (), s32[]{:S(2)}) async-start(), calls=%async_computation.21 | async-start | bytes 294912
  601.5 224.3 %reduce-scatter.30.cloned.1.call-start = ((), (), s32[]{:S(2)}) async-start(), calls=%async_computation.22 | async-start | bytes 294912
  602.4 292.6 %all-reduce.13.cloned.1.call-start = ((), (), s32[]{:S(2)}) async-start(), calls=%async_computation.24 | async-start | bytes 9437184
  649.1 4.4 copy-start.19
  664.5 4.0 copy-start.1
  664.5 4.0 copy-start.3
  664.5 4.0 copy-start.28
  668.5 3.0 copy-start.10
  682.5 3.0 copy-start.10
  696.4 3.0 copy-start.10
  710.3 3.0 copy-start.10
  731.6 6.8 copy-start.13
  762.9 2.7 copy-start.16
  775.9 205.2 %all-reduce.11.cloned.1.call-start = ((), (), s32[]{:S(2)}) async-start(), calls=%async_computation.23 | async-start | bytes 6291456
  785.8 1.9 copy-start.18
  785.8 275.1 %reduce-scatter.26.cloned.1.call-start = ((), (), s32[]{:S(2)}) async-start(), calls=%async_computation.20 | async-start | bytes 5013504 | tf_op jit(solution)/shard_map/reduce_scatter | solution.py:181
  797.4 1.9 copy-start.17
  797.4 343.0 %reduce-scatter.24.cloned.1.call-start = ((), (), s32[]{:S(2)}) async-start(), calls=%async_computation.19 | async-start | bytes 5013504 | tf_op jit(solution)/shard_map/reduce_scatter | solution.py:179
  808.9 2.0 copy-start.20
  808.9 8.5 copy-start.29
  808.9 392.6 %reduce-scatter.22.cloned.1.call-start = ((), (), s32[]{:S(2)}) async-start(), calls=%async_computation.18 | async-start | bytes 1253376 | tf_op jit(solution)/shard_map/reduce_scatter | solution.py:234
  815.1 7.5 copy-start.5
  824.7 5.7 copy-start.21
  824.7 156.4 %copy-start.9 = (f32[256,4,768]{2,1,0:T(4,128)S(1)}, f32[256,4,768]{2,1,0:T(4,128)}, u32[]{:S(2)}) copy-start(f32[256,4,768]{2,1,0:T(4,128)} %reshape.186) | copy-start | bytes 9437188
  (3 other events, 5.0 us)
Sparse Core Ops, SparseCore 0:
  9.6 47.6 all-gather.12
  59.5 40.3 all-gather.10
  215.4 42.3 reduce-scatter.15
  273.0 43.5 all-gather.14
  319.0 42.3 all-gather.16
  363.7 41.0 all-gather.18
  414.1 42.1 reduce-scatter.17
  469.3 44.9 all-gather.20
  547.5 43.3 reduce-scatter.19
  599.4 44.9 all-gather.22
  647.3 10.9 reduce-scatter.27
  660.4 10.9 reduce-scatter.29
  776.0 117.3 all-reduce.12
  895.6 85.4 all-reduce.10
  985.3 75.5 reduce-scatter.25
  1065.7 74.6 reduce-scatter.23
  1144.4 57.0 reduce-scatter.21
where the time goes:
time: 1220 us; the launch traced here: 1210 us
  waiting for transfers between devices  559 us (46%)
  local copies, waits for them, and re-layouts  206 us (17%)
  blocking collectives  181 us (15%)
  matrix products  179 us (15%)
  other arithmetic  63.4 us (5%)
  between operations  18.4 us (2%)
    unnamed x2, blocking collectives  92.3 us
    unnamed x21, waiting for transfers between devices  87 us
    reduce_scatter x1, waiting for transfers between devices, shards(): lax.psum_scatter(grad_w_in, 'dp', scatter_dimension=0, tiled=True)  79.5 us
    reduce_scatter x1, waiting for transfers between devices, shards(): lax.psum_scatter(grad_w_down, 'dp', scatter_dimension=1, tiled=True)  76 us
    reduce_scatter x1, waiting for transfers between devices, shards(): lax.psum_scatter(grad_w_out, 'dp', scatter_dimension=1, tiled=True)  61.1 us
    all_gather x1, waiting for transfers between devices, shards(): lax.all_gather(grad_second.astype(jnp.bfloat16).reshape(half_len, seq_cou...  45 us
    reduce_scatter x1, waiting for transfers between devices, shards(): lax.psum_scatter(jnp.einsum('tf,df->td', grad_before, w_in_all, preferred...  43.5 us
    all_gather x1, waiting for transfers between devices, shards(): lax.all_gather(grad_resid.astype(jnp.bfloat16).reshape(half_len, seq_coun...  41.9 us
  transfers between devices with their start and end apart: 17, of which 13 were waited for; matrix products, arithmetic and copies ran while one was open for 21% of the time, Pallas kernels for 0%

commit v1 on v0

v1 whole, which is shorter than its diff:
```python
import functools

import jax
import jax.numpy as jnp
from jax import lax
from jax.experimental import pallas as pl
from jax.experimental.pallas import tpu as pltpu
from jax.sharding import PartitionSpec as P

HEAD_DIM = 64
BOTH = ("dp", "tensor")
BIT_Y, BIT_CORE, BIT_X, BIT_Z = 1, 2, 4, 8
PLACES = 32

norm_eps = 1e-12
bf16 = jnp.bfloat16
f32 = jnp.float32


def norm_forward(values, gain, shift):
    centered = values - jnp.mean(values, axis=-1, keepdims=True)
    inverse = lax.rsqrt(jnp.mean(centered * centered, axis=-1, keepdims=True) + norm_eps)
    normed = centered * inverse
    return (normed * gain + shift, normed, inverse)


def norm_backward(grad, normed, inverse, gain):
    scaled = grad * gain
    inner = (
        scaled
        - jnp.mean(scaled, axis=-1, keepdims=True)
        - normed * jnp.mean(scaled * normed, axis=-1, keepdims=True)
    )
    return inner * inverse


def dot(left, right):
    return jnp.dot(left, right, preferred_element_type=f32)


def dot_nt(left, right):
    return lax.dot_general(left, right, (((1,), (1,)), ((), ())), preferred_element_type=f32)


def dot_tn(left, right):
    return lax.dot_general(left, right, (((0,), (0,)), ((), ())), preferred_element_type=f32)


def three_parts(value):
    high = value.astype(bf16)
    rest = value - high.astype(f32)
    middle = rest.astype(bf16)
    low = (rest - middle.astype(f32)).astype(bf16)
    return high.astype(f32), middle.astype(f32), low.astype(f32)


def key_bias(length, own, count):
    place = lax.broadcasted_iota(jnp.int32, (count, 128), 0)
    place = (place + own * (count // 2)) & (count - 1)
    return jnp.where(place < length, 0.0, -1000000000.0)


def attend_kernel(info_ref, q_ref, k_ref, v_ref, ctx_ref, lse_ref):
    count = q_ref.shape[0]
    lane = lax.broadcasted_iota(jnp.int32, (count, 128), 1)
    bias = key_bias(info_ref[1 + pl.program_id(0)], info_ref[0], count)
    query = q_ref[...].astype(f32) * (HEAD_DIM**-0.5)
    keys = k_ref[...].astype(f32)
    values = v_ref[...].astype(f32)
    contexts, sums = [], []
    for head in range(2):
        mine = (lane < 64) if head == 0 else (lane >= 64)
        extra = 64 * (1 - head)
        query_h = jnp.where(mine, query, jnp.where(lane == extra, 1.0, 0.0)).astype(bf16)
        keys_h = jnp.where(mine, keys, jnp.where(lane == extra, bias, 0.0)).astype(bf16)
        values_h = jnp.where(mine, values, 1.0).astype(bf16)
        scores = dot_nt(query_h, keys_h)
        peak = jnp.max(scores, axis=1, keepdims=True)
        exponent = jnp.exp(scores - peak).astype(bf16)
        mixed = dot(exponent, values_h)
        total = pltpu.roll(mixed, 64, 1)
        contexts.append(mixed / total)
        sums.append(peak + jnp.log(mixed))
    low = lane < 64
    ctx_ref[...] = jnp.where(low, contexts[0], contexts[1]).astype(bf16)
    lse_ref[...] = jnp.where(low, sums[1], sums[0])


def attend(info, qkv, seqs):
    rows, triple = qkv.shape
    count, pairs = rows // seqs, triple // 3 // 128
    block = lambda at: pl.BlockSpec((count, 128), lambda s, p, info: (s, p + at * pairs))
    return pl.pallas_call(
        attend_kernel,
        grid_spec=pltpu.PrefetchScalarGridSpec(
            num_scalar_prefetch=1,
            grid=(seqs, pairs),
            in_specs=[block(0), block(1), block(2)],
            out_specs=[block(0), block(0)],
        ),
        out_shape=[
            jax.ShapeDtypeStruct((rows, triple // 3), bf16),
            jax.ShapeDtypeStruct((rows, triple // 3), f32),
        ],
        compiler_params=pltpu.CompilerParams(vmem_limit_bytes=48 << 20),
        name="attend",
    )(info, qkv, qkv, qkv)


def attend_back_kernel(
    info_ref, q_ref, k_ref, v_ref, ctx_ref, lse_ref, dctx_ref, dq_ref, dk_ref, dv_ref
):
    count = q_ref.shape[0]
    lane = lax.broadcasted_iota(jnp.int32, (count, 128), 1)
    bias = key_bias(info_ref[1 + pl.program_id(0)], info_ref[0], count)
    scale = HEAD_DIM**-0.5
    query = q_ref[...].astype(f32) * scale
    query_low = query.astype(bf16)
    keys_low = k_ref[...]
    keys = keys_low.astype(f32)
    values = v_ref[...].astype(f32)
    grad_low = dctx_ref[...]
    grad = grad_low.astype(f32)
    product = grad * ctx_ref[...].astype(f32)
    lse_parts = three_parts(-lse_ref[...])
    outs = []
    for head in range(2):
        mine = (lane < 64) if head == 0 else (lane >= 64)
        at = lane - 64 * (1 - head)
        ones = jnp.where((at >= 1) & (at <= 3), 1.0, 0.0)

        def spread(parts, first):
            high, middle, low = parts
            value = jnp.where(at == 2, middle, jnp.where(at == 3, low, 0.0))
            return jnp.where(at == 1, high, jnp.where(at == 0, first, value))

        query_h = jnp.where(mine, query, spread(lse_parts, 1.0)).astype(bf16)
        keys_h = jnp.where(mine, keys, jnp.where(at == 0, bias, ones)).astype(bf16)
        inner = -jnp.sum(jnp.where(mine, product, 0.0), axis=1, keepdims=True)
        inner = jnp.broadcast_to(inner, (count, 128))
        grad_h = jnp.where(mine, grad, spread(three_parts(inner), 0.0)).astype(bf16)
        values_h = jnp.where(mine, values, ones).astype(bf16)
        probs = jnp.exp(dot_nt(keys_h, query_h))
        grad_probs = dot_nt(values_h, grad_h)
        grad_scores = (probs * grad_probs).astype(bf16)
        grad_values = dot(probs.astype(bf16), grad_low)
        grad_keys = dot(grad_scores, query_low)
        grad_query = dot_tn(grad_scores, keys_low) * scale
        outs.append((grad_query, grad_keys, grad_values))
    low = lane < 64
    for ref, first, second in zip((dq_ref, dk_ref, dv_ref), outs[0], outs[1]):
        ref[...] = jnp.where(low, first, second).astype(bf16)


def attend_back(info, qkv, ctx, lse, grad_ctx, seqs):
    rows, triple = qkv.shape
    count, pairs = rows // seqs, triple // 3 // 128
    block = lambda at: pl.BlockSpec((count, 128), lambda s, p, info: (s, p + at * pairs))
    return pl.pallas_call(
        attend_back_kernel,
        grid_spec=pltpu.PrefetchScalarGridSpec(
            num_scalar_prefetch=1,
            grid=(seqs, pairs),
            in_specs=[block(0), block(1), block(2), block(0), block(0), block(0)],
            out_specs=[block(0)] * 3,
        ),
        out_shape=[jax.ShapeDtypeStruct((rows, triple // 3), bf16)] * 3,
        compiler_params=pltpu.CompilerParams(vmem_limit_bytes=48 << 20),
        name="attend_back",
    )(info, qkv, qkv, qkv, ctx, lse, grad_ctx)


def gelu_and_slope(value):
    size = jnp.abs(value)
    near = 1.0 / (1.0 + (0.3275911 * 0.7071067811865476) * size)
    bell = jnp.exp(-0.5 * (value * value))
    poly = 0.5 * 1.061405429
    poly = poly * near + 0.5 * -1.453152027
    poly = poly * near + 0.5 * 1.421413741
    poly = poly * near + 0.5 * -0.284496736
    poly = poly * near + 0.5 * 0.254829592
    tail = poly * near * bell
    phi = jnp.where(value >= 0, 1.0 - tail, tail)
    return value * phi, phi + value * (bell * 0.3989422804014327)


def up_kernel(h_ref, w_ref, b_ref, g_ref, s_ref):
    rows = h_ref.shape[0]
    step = 256
    for at in range(0, rows, step):
        part = pl.ds(at, step)
        before = dot(h_ref[part, :], w_ref[...]) + b_ref[...]
        hidden, slope = gelu_and_slope(before)
        g_ref[part, :] = hidden.astype(bf16)
        s_ref[part, :] = slope.astype(bf16)


def up(first_low, w_in, b_in):
    rows, width = first_low.shape
    units = w_in.shape[1]
    step = 512
    return pl.pallas_call(
        up_kernel,
        grid=(units // step,),
        in_specs=[
            pl.BlockSpec((rows, width), lambda i: (0, 0)),
            pl.BlockSpec((width, step), lambda i: (0, i)),
            pl.BlockSpec((1, step), lambda i: (0, i)),
        ],
        out_specs=[pl.BlockSpec((rows, step), lambda i: (0, i))] * 2,
        out_shape=[jax.ShapeDtypeStruct((rows, units), bf16)] * 2,
        compiler_params=pltpu.CompilerParams(vmem_limit_bytes=48 << 20),
        name="up",
    )(first_low, w_in, b_in)


def swap(value, even, odd):
    pairs = [(i, i ^ (odd if i & BIT_CORE else even)) for i in range(PLACES)]
    return lax.ppermute(value, BOTH, pairs)


def gather_parts(shard):
    group = jnp.stack([shard] + [swap(shard, BIT_Z * k, BIT_Z * k) for k in (1, 2, 3)])
    near = swap(group, BIT_X, BIT_Y)
    far = swap(group, BIT_Y, BIT_X)
    corner = swap(near, BIT_Y, BIT_X)
    own = [group, near, far, corner]
    return own + [swap(part, BIT_CORE, BIT_CORE) for part in own]


def scatter_parts(mine, theirs):
    total = mine.astype(f32) + swap(theirs, BIT_CORE, BIT_CORE).astype(f32)
    far = swap(total[2].astype(bf16), BIT_Y, BIT_X).astype(f32)
    corner = swap(total[3].astype(bf16), BIT_Y, BIT_X).astype(f32)
    near = swap((total[1] + corner).astype(bf16), BIT_X, BIT_Y).astype(f32)
    group = total[0] + far + near
    result = group[0]
    for k in (1, 2, 3):
        result = result + swap(group[k].astype(bf16), BIT_Z * k, BIT_Z * k).astype(f32)
    return result


def slots(me):
    core = (me >> 1) & 1
    for other in (0, 1):
        along = jnp.where((core ^ other) == 0, BIT_X, BIT_Y)
        across = (BIT_X + BIT_Y) - along
        for part, bits in enumerate((0, along, across, BIT_X + BIT_Y)):
            for k in range(4):
                yield other, part, k, me ^ (other * BIT_CORE) ^ bits ^ (k * BIT_Z)


def window(ref, move, place):
    _, rows, columns, _, step, start, wide = move
    row = pl.multiple_of((place >> 1 if wide else place) * step, 16)
    if not wide:
        return ref.at[pl.ds(row, rows), :]
    column = pl.multiple_of(start + (place & 1) * columns, 128)
    return ref.at[pl.ds(row, rows), pl.ds(column, columns)]


def place_kernel(me_ref, *refs, moves, outs):
    ins, wholes, sems = refs[:8], refs[8 : 8 + outs], refs[8 + outs]
    for other, part, k, place in slots(me_ref[0]):
        for move in moves:
            source, rows, to = move[0], move[1], move[3]
            pltpu.make_async_copy(
                ins[4 * other + part].at[k, pl.ds(source, rows), :],
                window(wholes[to], move, place),
                sems.at[to],
            ).start()
    for to in range(outs):
        pltpu.make_async_copy(wholes[to], wholes[to], sems.at[to]).wait()


def spread_kernel(me_ref, *refs, moves, ins):
    wholes, halves, sems = refs[:ins], refs[ins : ins + 2], refs[ins + 2]
    for other, part, k, place in slots(me_ref[0]):
        for move in moves:
            source, rows, to = move[0], move[1], move[3]
            pltpu.make_async_copy(
                window(wholes[to], move, place),
                halves[other].at[part, k, pl.ds(source, rows), :],
                sems.at[other],
            ).start()
    for other in (0, 1):
        pltpu.make_async_copy(halves[other], halves[other], sems.at[other]).wait()


anywhere = pl.BlockSpec(memory_space=pl.ANY)
on_core = pl.BlockSpec(memory_space=pltpu.VMEM)


def place(me, parts, moves, shapes):
    return pl.pallas_call(
        functools.partial(place_kernel, moves=moves, outs=len(shapes)),
        in_specs=[pl.BlockSpec(memory_space=pltpu.SMEM)] + [anywhere] * 8,
        out_specs=[on_core] * len(shapes),
        out_shape=[jax.ShapeDtypeStruct(shape, bf16) for shape in shapes],
        compiler_params=pltpu.CompilerParams(vmem_limit_bytes=48 << 20),
        scratch_shapes=[pltpu.SemaphoreType.DMA((len(shapes),))],
        name="place",
    )(me, *parts)


def spread(me, wholes, moves, rows, columns):
    return pl.pallas_call(
        functools.partial(spread_kernel, moves=moves, ins=len(wholes)),
        in_specs=[pl.BlockSpec(memory_space=pltpu.SMEM)] + [anywhere] * len(wholes),
        out_specs=[on_core] * 2,
        out_shape=[jax.ShapeDtypeStruct((4, 4, rows, columns), bf16)] * 2,
        compiler_params=pltpu.CompilerParams(vmem_limit_bytes=48 << 20),
        scratch_shapes=[pltpu.SemaphoreType.DMA((2,))],
        name="spread",
    )(me, *wholes)


def move_list(row, blocks, vectors):
    moves, at = [], 0
    for to, columns, starts in blocks:
        for start in starts:
            moves.append((at, row, columns, to, row, start, True))
            at += row
    if vectors:
        moves.append((at, 16, blocks[0][1], vectors, 16, 0, False))
    return tuple(moves)


def gather_whole(me, shard, moves, shapes, direct):
    if direct:
        return place(me, gather_parts(shard), moves, shapes)
    everything = lax.all_gather(shard, BOTH, axis=0)
    places = everything.shape[0]
    wholes = [jnp.zeros((0,), bf16)] * len(shapes)
    for to, shape in enumerate(shapes):
        pieces = []
        for source, rows, columns, at, _, _, wide in moves:
            if at != to:
                continue
            piece = everything[:, source : source + rows]
            if wide:
                piece = piece.reshape(places // 2, 2, rows, columns).transpose(0, 2, 1, 3)
                pieces.append(piece.reshape(places // 2 * rows, 2 * columns))
            else:
                pieces.append(piece.reshape(shape))
        wholes[to] = jnp.concatenate(pieces, axis=1)
    return wholes


def scatter_whole(me, wholes, moves, rows, columns, direct):
    if direct:
        return scatter_parts(*spread(me, wholes, moves, rows, columns))
    pieces = []
    for _, count, wide_columns, to, step, start, wide in moves:
        whole = wholes[to]
        if wide:
            whole = whole[:, start : start + 2 * wide_columns]
            whole = whole.reshape(-1, count, 2, wide_columns).transpose(0, 2, 1, 3)
        pieces.append(whole.reshape(-1, count, wide_columns))
    return lax.psum_scatter(
        jnp.concatenate(pieces, axis=1), BOTH, scatter_dimension=0, tiled=True
    )[0].astype(f32)


def shards(
    tokens, lengths, w_qkv, qkv_bias, w_out, w_in, b_in, w_down, norm_gains, row_biases, cotangent, direct
):
    half_len, seq_count, width = tokens.shape
    own = lax.axis_index("tensor")
    me = (lax.axis_index("dp") * 2 + own).astype(jnp.int32).reshape(1)
    seqs = seq_count // 2
    row = w_qkv.shape[1]
    local_width, local_units = w_qkv.shape[2], w_in.shape[1]
    count = qkv_bias.shape[1]
    units = 2 * local_units
    places = width // row * 2
    total_rows = seqs * 2 * half_len

    def trade(value):
        return lax.ppermute(value, "tensor", [(0, 1), (1, 0)])

    def to_rows(value):
        by_seq = jnp.swapaxes(value, 0, 1)
        kept = lax.dynamic_slice_in_dim(by_seq, own * seqs, seqs, 0)
        sent = lax.dynamic_slice_in_dim(by_seq, (1 - own) * seqs, seqs, 0)
        return jnp.stack([kept, trade(sent)], axis=1).reshape(total_rows, width)

    def from_rows(value, kind):
        halves = value.reshape(seqs, 2, half_len, width)
        kept = halves[:, 0]
        got = trade(halves[:, 1].astype(bf16)).astype(value.dtype)
        first = jnp.where(own == 0, kept, got)
        second = jnp.where(own == 0, got, kept)
        return jnp.swapaxes(jnp.concatenate([first, second], axis=0), 0, 1).astype(kind)

    def pack(pieces, kind):
        flat = jnp.concatenate([piece.reshape(piece.shape[0], -1) for piece in pieces], axis=1)
        flat = jnp.pad(flat, ((0, 0), (0, local_width - flat.shape[1])))
        return jnp.pad(flat[:, None, :], ((0, 0), (0, 15), (0, 0))).astype(kind)

    rows = to_rows(tokens)
    vectors = pack(
        [qkv_bias[None], b_in[None], norm_gains[None], row_biases[None]], bf16
    ).reshape(16, local_width)
    attn_shard = jnp.concatenate([w_qkv.reshape(3 * row, local_width), w_out.T, vectors], axis=0)
    qkv_starts = (0, width, 2 * width)
    attn_moves = move_list(row, [(0, local_width, qkv_starts), (1, local_width, (0,))], 2)
    wq, wo, vector_rows = gather_whole(
        me,
        attn_shard,
        attn_moves,
        [(width, 3 * width), (width, width), (places * 16, local_width)],
        direct,
    )
    mlp_moves = move_list(row, [(0, local_units, (0,))], None)
    (wi,) = gather_whole(me, w_in, mlp_moves, [(width, units)], direct)
    (wd,) = gather_whole(me, w_down.T, mlp_moves, [(width, units)], direct)

    flat = vector_rows.reshape(places // 2, 2, 16, local_width)[:, :, 0]
    flat = jnp.swapaxes(flat, 0, 1).reshape(places, local_width)

    def vector(at, lines, size):
        piece = flat[:, at : at + lines * size].reshape(places, lines, size)
        return jnp.swapaxes(piece, 0, 1).reshape(lines, places * size)

    wide = b_in.shape[0]
    bias_pair = vector(0, 2, count)
    b_in_all = vector(2 * count, 1, wide)
    gains = vector(2 * count + wide, 2, count).astype(f32)
    shifts = vector(4 * count + wide, 4, count).astype(f32)

    mine_lengths = lax.dynamic_slice_in_dim(lengths, own * seqs, seqs, 0)
    info = jnp.concatenate([own.reshape(1).astype(jnp.int32), mine_lengths])

    qkv_shift = jnp.concatenate([bias_pair[0], jnp.zeros((width,), bf16), bias_pair[1]])
    qkv = (dot(rows, wq) + qkv_shift.astype(f32)).astype(bf16)
    ctx, lse = attend(info, qkv, seqs)
    attended = dot_nt(ctx, wo)
    first, normed_one, inverse_one = norm_forward(
        rows.astype(f32) + attended + shifts[0], gains[0], shifts[1]
    )
    first_low = first.astype(bf16)
    hidden, slope = up(first_low, wi, b_in_all.astype(f32))
    mixed = dot_nt(hidden, wd)
    output, normed_two, inverse_two = norm_forward(first + mixed + shifts[2], gains[1], shifts[3])
    out = from_rows(output.astype(bf16), bf16)

    grad_output = to_rows(cotangent).astype(f32)
    grad_gain_two = jnp.sum(grad_output * normed_two, axis=0)
    grad_shift_two = jnp.sum(grad_output, axis=0)
    grad_second = norm_backward(grad_output, normed_two, inverse_two, gains[1])
    grad_down_bias = jnp.sum(grad_second, axis=0)
    mixed_grad = grad_second.astype(bf16)
    grad_wd = dot_tn(mixed_grad, hidden).astype(bf16)
    grad_down = scatter_whole(me, [grad_wd], mlp_moves, row, local_units, direct).T
    grad_before = (dot(mixed_grad, wd) * slope.astype(f32)).astype(bf16)
    grad_in_bias = jnp.sum(grad_before, axis=0, dtype=f32)
    grad_wi = dot_tn(first_low, grad_before).astype(bf16)
    grad_in = scatter_whole(me, [grad_wi], mlp_moves, row, local_units, direct)
    grad_first = dot_nt(grad_before, wi) + grad_second
    grad_gain_one = jnp.sum(grad_first * normed_one, axis=0)
    grad_shift_one = jnp.sum(grad_first, axis=0)
    grad_resid = norm_backward(grad_first, normed_one, inverse_one, gains[0])
    grad_out_bias = jnp.sum(grad_resid, axis=0)
    attn_grad = grad_resid.astype(bf16)
    grad_wo = dot_tn(attn_grad, ctx).astype(bf16)
    out_moves = move_list(row, [(0, local_width, (0,))], None)
    grad_out = scatter_whole(me, [grad_wo], out_moves, row, local_width, direct).T
    grad_ctx = dot(attn_grad, wo).astype(bf16)
    grad_query, grad_keys, grad_values = attend_back(info, qkv, ctx, lse, grad_ctx, seqs)
    grad_triple = jnp.concatenate([grad_query, grad_keys, grad_values], axis=1)
    grad_wq = dot_tn(rows, grad_triple).astype(bf16)

    def shares(value, lines):
        size = value.size // lines // places
        piece = value.reshape(lines, 2, places // 2, size)
        return piece.transpose(2, 1, 0, 3).reshape(places, lines * size)

    grad_pair = jnp.stack(
        [jnp.sum(grad_query, axis=0, dtype=f32), jnp.sum(grad_values, axis=0, dtype=f32)]
    )
    grad_vectors = pack(
        [
            shares(grad_pair, 2),
            shares(grad_in_bias, 1),
            shares(jnp.stack([grad_gain_one, grad_gain_two]), 2),
            shares(
                jnp.stack([grad_out_bias, grad_shift_one, grad_down_bias, grad_shift_two]), 4
            ),
        ],
        bf16,
    ).reshape(places * 16, local_width)
    qkv_moves = move_list(row, [(0, local_width, qkv_starts)], 1)
    attn_piece = scatter_whole(
        me, [grad_wq, grad_vectors], qkv_moves, 3 * row + 16, local_width, direct
    )
    grad_qkv = attn_piece[: 3 * row].reshape(3, row, local_width)
    line = attn_piece[3 * row]
    grad_tokens = dot_nt(grad_triple, wq) + grad_resid
    d_tokens = from_rows(grad_tokens, f32)

    def cut(at, lines, size):
        return line[at : at + lines * size].reshape(lines, size)

    return (
        out,
        d_tokens,
        grad_qkv,
        cut(0, 2, count),
        grad_out,
        grad_in,
        cut(2 * count, 1, wide)[0],
        grad_down,
        cut(2 * count + wide, 2, count),
        cut(4 * count + wide, 4, count),
    )


def solution(mesh):
    placed = (
        P("tensor", "dp", None),
        P("dp"),
        P(None, "dp", "tensor"),
        P(None, ("tensor", "dp")),
        P("tensor", "dp"),
        P("dp", "tensor"),
        P(("tensor", "dp")),
        P("tensor", "dp"),
        P(None, ("tensor", "dp")),
        P(None, ("tensor", "dp")),
        P("tensor", "dp", None),
    )
    direct = mesh.shape["tensor"] == 2 and mesh.shape["dp"] * 2 == PLACES
    return jax.shard_map(
        functools.partial(shards, direct=direct),
        mesh=mesh,
        in_specs=placed,
        out_specs=(
            P("tensor", "dp", None),
            P("tensor", "dp", None),
            P(None, "dp", "tensor"),
            P(None, ("tensor", "dp")),
            P("tensor", "dp"),
            P("dp", "tensor"),
            P(("tensor", "dp")),
            P("tensor", "dp"),
            P(None, ("tensor", "dp")),
            P(None, ("tensor", "dp")),
        ),
        check_vma=False,
    )
```

time: 1220 us -> 486 us (0.40)
  waiting for transfers between devices: 559 us -> 131 us
  blocking collectives: 181 us -> 0 us
  local copies, waits for them, and re-layouts: 206 us -> 62.5 us
  matrix products: 179 us -> 71.3 us
  Pallas kernels: 0 us -> 81.2 us
  starting transfers between devices: 0.94 us -> 70.6 us
  between operations: 18.4 us -> 2.02 us
    reduce_scatter x6 -> x0, waiting for transfers between devices: 295 us -> none  [the longest x1 79.5 us: shards(): lax.psum_scatter(grad_w_in, 'dp', scatter_dimension=0, tiled=True)]
    all_gather x7 -> x0, waiting for transfers between devices: 177 us -> none  [the longest x1 45 us: shards(): lax.all_gather(grad_second.astype(jnp.bfloat16).reshape(half_len, seq_cou...]
    ppermute x0 -> x62, waiting for transfers between devices: none -> 131 us  [the longest x58 121 us: swap(): return lax.ppermute(value, BOTH, pairs)]
    dot_general x40 -> x11, matrix products: 179 us -> 71.3 us  [the longest x4 28.7 us: dot_tn(): lax.dot_general(left, right, (((0,), (0,)), ((), ())), preferred_element_...]
    unnamed x2 -> x0, blocking collectives: 92.3 us -> none
    all_gather x6 -> x0, blocking collectives: 88.8 us -> none  [the longest x1 23.1 us: shards(): lax.all_gather(qkv_bias, 'dp', axis=1, tiled=True)]
    unnamed x21 -> x0, waiting for transfers between devices: 87 us -> none
    pallas_call x0 -> x10, Pallas kernels: none -> 81.2 us  [the longest x1 24.5 us: attend_back(): pl.pallas_call(attend_back_kernel, grid_spec=pltpu.PrefetchScalarGridSpec...]
  transfers between devices with their start and end apart: 17 -> 62, of which waited for: 13 -> 18; matrix products, arithmetic and copies ran while one was open for 21% -> 18% of each run, Pallas kernels for 0% -> 3%
where the time goes in v1:
time: 486 us; the launch traced here: 477 us
  waiting for transfers between devices  131 us (27%)
  Pallas kernels  81.2 us (17%)
  matrix products  71.3 us (15%)
  starting transfers between devices  70.6 us (15%)
  local copies, waits for them, and re-layouts  62.5 us (13%)
  other arithmetic  57.6 us (12%)
    ppermute x58, waiting for transfers between devices, swap(): return lax.ppermute(value, BOTH, pairs)  121 us
    ppermute x58, starting transfers between devices, swap(): return lax.ppermute(value, BOTH, pairs)  65.1 us
    unnamed x128, local copies, waits for them, and re-layouts  28.9 us
    dot_general x4, matrix products, dot_tn(): lax.dot_general(left, right, (((0,), (0,)), ((), ())), preferred_element_...  28.7 us
    pallas_call x1, Pallas kernels, attend_back(): pl.pallas_call(attend_back_kernel, grid_spec=pltpu.PrefetchScalarGridSpec...  24.5 us
    dot_general x4, matrix products, dot_nt(): lax.dot_general(left, right, (((1,), (1,)), ((), ())), preferred_element_...  23.9 us
    dot_general x3, matrix products, dot(): return jnp.dot(left, right, preferred_element_type=f32)  18.7 us
    pallas_call x1, Pallas kernels, up(): pl.pallas_call(up_kernel, grid=(units // step,), in_specs=[pl.BlockSpec((...  17.4 us
  transfers between devices with their start and end apart: 62, of which 18 were waited for; matrix products, arithmetic and copies ran while one was open for 18% of the time, Pallas kernels for 3%

profile of v1, /device:TPU:0, one launch (start us, length us, event | category | flops | bytes accessed | tf_op | source)
XLA Modules:
  0.0 476.5 jit_solution(15243869019866741609)
XLA Ops:
  0.6 3.1 collective-permute-start.11
  3.7 2.6 collective-permute-start.12
  7.2 3.5 collective-permute-start.22
  15.5 2.5 collective-permute-done.12
  22.0 8.6 %collective-permute-done.22 = bf16[48,1536]{1,0:T(8,128)(2,1)S(1)} collective-permute-done((bf16[48,1536]{1,0:T(8,128)(2,1)}, bf16[48,1536]{1,0:T(8,128)(2,1)S(1)}, u32[]{:S(2)}, u32[]{:S(2)}) %collective-permute-start.22) | collective-permute-done | bytes 147488 | tf_op jit(solution)/shard_map/ppermute | solution.py:219
  34.5 4.9 %fusion.67 = (bf16[768]{0:T(1024)(128)(2,1)S(1)}, bf16[256,2,768]{2,1,0:T(2,128)(2,1)}, bf16[256,2,768]{2,1,0:T(2,128)(2,1)S(1)}) fusion(bf16[256,4,768]{2,1,0:T(4,128)(2,1)} %param.21, s32[]{:T(128)S(6)} %select_n.32, s32[]{:T(128)S(6)} %select_n.33), kind=kLoop, calls=%fused_computation.178 | loop fusion | flops 392448 | bytes 3147272 | tf_op jit(solution)/shard_map/reduce_sum | solution.py:450
  39.5 4.4 dynamic-slice_bitcast_fusion.1
  49.4 12.5 %collective-permute-done.24.refs_1_ = bf16[4,48,1536]{2,1,0:T(8,128)(2,1)S(1)} collective-permute-done((bf16[4,48,1536]{2,1,0:T(8,128)(2,1)S(1)}, bf16[4,48,1536]{2,1,0:T(8,128)(2,1)S(1)}, u32[]{:S(2)}, u32[]{:S(2)}) %collective-permute-start.24) | collective-permute-done | bytes 589856 | tf_op jit(solution)/shard_map/ppermute | solution.py:219
  63.7 29.6 %collective-permute-done.25.refs_2_ = bf16[4,48,1536]{2,1,0:T(8,128)(2,1)S(1)} collective-permute-done((bf16[4,48,1536]{2,1,0:T(8,128)(2,1)S(1)}, bf16[4,48,1536]{2,1,0:T(8,128)(2,1)S(1)}, u32[]{:S(2)}, u32[]{:S(2)}) %collective-permute-start.25) | collective-permute-done | bytes 589856 | tf_op jit(solution)/shard_map/ppermute | solution.py:219
  98.4 10.9 %collective-permute-done.5.refs_2_ = bf16[4,208,384]{2,1,0:T(8,128)(2,1)S(1)} collective-permute-done((bf16[4,208,384]{2,1,0:T(8,128)(2,1)S(1)}, bf16[4,208,384]{2,1,0:T(8,128)(2,1)S(1)}, u32[]{:S(2)}, u32[]{:S(2)}) %collective-permute-start.5) | collective-permute-done | bytes 639008 | tf_op jit(solution)/shard_map/ppermute | solution.py:219
  111.0 4.6 collective-permute-done.16.refs_3_
  120.4 8.6 %collective-permute-done.26.refs_3_ = bf16[4,48,1536]{2,1,0:T(8,128)(2,1)} collective-permute-done((bf16[4,48,1536]{2,1,0:T(8,128)(2,1)S(1)}, bf16[4,48,1536]{2,1,0:T(8,128)(2,1)}, u32[]{:S(2)}, u32[]{:S(2)}) %collective-permute-start.26) | collective-permute-done | bytes 589856 | tf_op jit(solution)/shard_map/ppermute | solution.py:219
  134.8 3.7 pad_maximum_fusion
  149.3 3.5 place.4.w_ref
  152.9 4.2 place.5
  157.1 4.7 place.3
  163.0 8.6 %add_convert_fusion.q_ref.k_ref.v_ref = bf16[1024,2304]{1,0:T(8,128)(2,1)} fusion(bf16[1024,768]{1,0:T(8,128)(2,1)} %bitcast.274, bf16[768,2304]{1,0:T(8,128)(2,1)} %get-tuple-element.28, f32[2304]{0:T(1024)S(1)} %maximum_convert_fusion), kind=kOutput, calls=%fused_computation.1 | convolution fusion | flops 3628597248 | bytes 9839616 | tf_op jit(solution)/shard_map/dot_general | solution.py:38
  171.5 16.6 %attend.1 = (bf16[1024,768]{1,0:T(8,128)(2,1)S(1)}, f32[1024,768]{1,0:T(8,128)S(1)}) custom-call(s32[3]{0:T(128)S(1)} %pad_add_fusion.info_ref, bf16[1024,2304]{1,0:T(8,128)(2,1)} %add_convert_fusion.q_ref.k_ref.v_ref, bf16[1024,2304]{1,0:T(8,128)(2,1)} %add_convert_fusion.q_ref.k_ref.v_ref, bf16[1024,2304]{1,0:T(8,128)(2,1)} %add_convert_fusion.q_ref.k_ref.v_ref), custom_call_target="tpu_custom_call" | custom-call | tf_op jit(solution)/shard_map/attend/pallas_call | solution.py:93
  194.9 17.4 %up.1 = (bf16[1024,3072]{1,0:T(8,128)(2,1)}, bf16[1024,3072]{1,0:T(8,128)(2,1)}) custom-call(bf16[1024,768]{1,0:T(8,128)(2,1)S(1)} %fusion.7.h_ref, bf16[768,3072]{1,0:T(8,128)(2,1)} %place.4.w_ref, f32[1,3072]{1,0:T(1,128)S(1)} %reshape.276.b_ref), custom_call_target="tpu_custom_call" | custom-call | tf_op jit(solution)/shard_map/up/pallas_call | solution.py:202
  212.3 9.4 %fusion.75 = (f32[1024]{0:T(1024)S(1)}, f32[1024,768]{1,0:T(8,128)S(1)}) fusion(f32[768]{0:T(1024)S(1)} %add.194, bf16[1024,3072]{1,0:T(8,128)(2,1)} %get-tuple-element.32, bf16[768,3072]{1,0:T(8,128)(2,1)} %place.5, f32[768]{0:T(1024)S(1)} %add.190, f32[768]{0:T(1024)S(1)} %mul.120, f32[1024]{0:T(1024)S(1)} %add_rsqrt_fusion.1, ...), kind=kOutput, calls=%fused_computation.186 | convolution fusion | flops 4837342208 | bytes 17323008 | tf_op jit(solution)/shard_map/dot_general | solution.py:42
  225.8 3.7 fusion.6
  229.6 4.7 fusion.65
  234.4 9.7 %convolution_convert_fusion.refs_0_ = bf16[768,3072]{1,0:T(8,128)(2,1)} fusion(bf16[1024,3072]{1,0:T(8,128)(2,1)} %get-tuple-element.32, f32[1024,768]{1,0:T(8,128)S(1)} %get-tuple-element.69), kind=kOutput, calls=%fused_computation.2 | convolution fusion | flops 4834983936 | bytes 14155776 | tf_op jit(solution)/shard_map/dot_general | solution.py:46
  244.1 7.6 %fusion.76 = (bf16[3072]{0:T(1024)(128)(2,1)}, bf16[1024,3072]{1,0:T(8,128)(2,1)}) fusion(bf16[1024,3072]{1,0:T(8,128)(2,1)S(1)} %bitcast.307, bf16[768,3072]{1,0:T(8,128)(2,1)S(1)} %bitcast.271, f32[1024,768]{1,0:T(8,128)S(1)} %get-tuple-element.69), kind=kOutput, calls=%fused_computation.187 | convolution fusion | flops 4845204480 | bytes 20453376 | tf_op jit(solution)/shard_map/dot_general | solution.py:38
  251.8 9.7 %convolution_convert_fusion.1.refs_0_ = bf16[768,3072]{1,0:T(8,128)(2,1)} fusion(bf16[1024,768]{1,0:T(8,128)(2,1)S(1)} %fusion.7.h_ref, bf16[1024,3072]{1,0:T(8,128)(2,1)} %get-tuple-element.132), kind=kOutput, calls=%fused_computation.3 | convolution fusion | flops 4834197504 | bytes 12582912 | tf_op jit(solution)/shard_map/dot_general | solution.py:46
  261.5 9.1 %multiply_reduce_fusion = (bf16[768]{0:T(1024)(128)(2,1)}, f32[1024]{0:T(1024)S(1)}, f32[1024]{0:T(1024)S(1)}, bf16[768]{0:T(1024)(128)(2,1)}, f32[1024,768]{1,0:T(8,128)S(1)}) fusion(f32[1024,768]{1,0:T(8,128)S(1)} %copy-done.30, f32[1024]{0:T(1024)S(1)} %add_rsqrt_fusion.1, f32[1024]{0:T(1024)S(1)} %broadcast_multiply_fusion.4, f32[768]{0:T(1024)S(1)} %mul.120, ...), kind=kOutput, calls=%fused_computation.19 | convolution fusion | flops 4839698432 | bytes 20469760 | tf_op jit(solution)/shard_map/dot_general | solution.py:42
  273.9 2.5 convolution_convert_fusion.3.dctx_ref
  276.4 24.5 %attend_back.1 = (bf16[1024,768]{1,0:T(8,128)(2,1)S(1)}, bf16[1024,768]{1,0:T(8,128)(2,1)S(1)}, bf16[1024,768]{1,0:T(8,128)(2,1)S(1)}) custom-call(s32[3]{0:T(128)S(1)} %pad_add_fusion.info_ref, bf16[1024,2304]{1,0:T(8,128)(2,1)} %add_convert_fusion.q_ref.k_ref.v_ref, bf16[1024,2304]{1,0:T(8,128)(2,1)} %add_convert_fusion.q_ref.k_ref.v_ref, ...), custom_call_target="tpu_custom_call" | custom-call | tf_op jit(solution)/shard_map/attend_back/pallas_call | solution.py:159
  302.4 2.7 copy-done.49
  305.2 3.9 convolution_add_fusion.1
  311.3 3.9 spread.7
  317.0 3.8 spread.6
  329.6 2.5 fusion.70
  336.2 7.7 %convolution_convert_fusion.2.refs_0_ = bf16[768,2304]{1,0:T(8,128)(2,1)} fusion(bf16[1024,768]{1,0:T(8,128)(2,1)S(1)} %bitcast.276, bf16[1024,2304]{1,0:T(8,128)(2,1)} %copy-done.40), kind=kOutput, calls=%fused_computation.4 | convolution fusion | flops 3625648128 | bytes 9830400 | tf_op jit(solution)/shard_map/dot_general | solution.py:46
  362.6 2.7 broadcast_select_fusion.1
  365.3 10.7 %collective-permute-done.33 = bf16[2,256,768]{2,0,1:T(2,128)(2,1)S(1)} collective-permute-done((bf16[2,256,768]{2,0,1:T(2,128)(2,1)S(1)}, bf16[2,256,768]{2,0,1:T(2,128)(2,1)S(1)}, u32[]{:S(2)}, u32[]{:S(2)}) %collective-permute-start.33) | collective-permute-done | bytes 786464 | tf_op jit(solution)/shard_map/ppermute | solution.py:380
  378.4 2.8 collective-permute-done.44
  381.2 8.0 %collective-permute-start.45 = (bf16[48,384]{1,0:T(8,128)(2,1)S(1)}, bf16[48,384]{1,0:T(8,128)(2,1)S(1)}, u32[]{:S(2)}, u32[]{:S(2)}) collective-permute-start(bf16[48,384]{1,0:T(8,128)(2,1)S(1)} %get-tuple-element.115), channel_id=1, source_target_pairs={{0,8},{1,9},{2,10},{3,11},{4,12},{5,13},{6,14},{7,15},{8,0},{9,1},... | collective-permute-start | bytes 110600 | tf_op jit(solution)/shard_map/ppermute | solution.py:219
  389.2 3.1 maximum_bitcast_fusion
  394.7 2.8 maximum_bitcast_fusion.1
  401.6 2.6 fusion.55
  406.4 2.6 fusion.54
  410.4 8.5 %collective-permute-done.35 = bf16[4,160,384]{2,1,0:T(8,128)(2,1)S(1)} collective-permute-done((bf16[4,160,384]{2,1,0:T(8,128)(2,1)S(1)}, bf16[4,160,384]{2,1,0:T(8,128)(2,1)S(1)}, u32[]{:S(2)}, u32[]{:S(2)}) %collective-permute-start.35) | collective-permute-done | bytes 491552 | tf_op jit(solution)/shard_map/ppermute | solution.py:219
  418.9 4.5 collective-permute-done.37
  429.0 9.1 %collective-permute-done.50 = bf16[4,48,1536]{2,1,0:T(8,128)(2,1)S(1)} collective-permute-done((bf16[4,48,1536]{2,1,0:T(8,128)(2,1)S(1)}, bf16[4,48,1536]{2,1,0:T(8,128)(2,1)S(1)}, u32[]{:S(2)}, u32[]{:S(2)}) %collective-permute-start.50) | collective-permute-done | bytes 589856 | tf_op jit(solution)/shard_map/ppermute | solution.py:219
  444.6 5.7 %collective-permute-done.58 = bf16[4,48,1536]{2,1,0:T(8,128)(2,1)} collective-permute-done((bf16[4,48,1536]{2,1,0:T(8,128)(2,1)}, bf16[4,48,1536]{2,1,0:T(8,128)(2,1)}, u32[]{:S(2)}, u32[]{:S(2)}) %collective-permute-start.58) | collective-permute-done | bytes 589856 | tf_op jit(solution)/shard_map/ppermute | solution.py:219
  463.7 3.6 collective-permute-done.52
  467.3 8.1 %collective-permute-done.53 = bf16[48,1536]{1,0:T(8,128)(2,1)S(1)} collective-permute-done((bf16[48,1536]{1,0:T(8,128)(2,1)S(1)}, bf16[48,1536]{1,0:T(8,128)(2,1)S(1)}, u32[]{:S(2)}, u32[]{:S(2)}) %collective-permute-start.53) | collective-permute-done | bytes 147488 | tf_op jit(solution)/shard_map/ppermute | solution.py:219
  (342 shorter events, 139.7 us)
Async XLA Ops:
  0.6 14.0 %collective-permute-start.11 = (bf16[48,1536]{1,0:T(8,128)(2,1)}, bf16[48,1536]{1,0:T(8,128)(2,1)S(1)}, u32[]{:S(2)}, u32[]{:S(2)}) collective-permute-start(bf16[48,1536]{1,0:T(8,128)(2,1)} %param.16), channel_id=1, source_target_pairs={{0,8},{1,9},{2,10},{3,11},{4,12},{5,13},{6,14},{7,15},{8,0},{9,1},... | collective-permute-start | bytes 442376 | tf_op jit(solution)/shard_map/ppermute | solution.py:219
  3.7 14.2 %collective-permute-start.12 = (bf16[48,1536]{1,0:T(8,128)(2,1)}, bf16[48,1536]{1,0:T(8,128)(2,1)S(1)}, u32[]{:S(2)}, u32[]{:S(2)}) collective-permute-start(bf16[48,1536]{1,0:T(8,128)(2,1)} %param.16), channel_id=1, source_target_pairs={{0,16},{1,17},{2,18},{3,19},{4,20},{5,21},{6,22},{7,23},{8,24},{9,... | collective-permute-start | bytes 442376 | tf_op jit(solution)/shard_map/ppermute | solution.py:219
  6.3 14.2 %collective-permute-start.21 = (bf16[48,1536]{1,0:T(8,128)(2,1)}, bf16[48,1536]{1,0:T(8,128)(2,1)S(1)}, u32[]{:S(2)}, u32[]{:S(2)}) collective-permute-start(bf16[48,1536]{1,0:T(8,128)(2,1)} %bitcast.286), channel_id=1, source_target_pairs={{0,8},{1,9},{2,10},{3,11},{4,12},{5,13},{6,14},{7,15},{8,0},{9,1},... | collective-permute-start | bytes 442376 | tf_op jit(solution)/shard_map/ppermute | solution.py:219
  7.2 23.4 %collective-permute-start.22 = (bf16[48,1536]{1,0:T(8,128)(2,1)}, bf16[48,1536]{1,0:T(8,128)(2,1)S(1)}, u32[]{:S(2)}, u32[]{:S(2)}) collective-permute-start(bf16[48,1536]{1,0:T(8,128)(2,1)} %bitcast.287), channel_id=1, source_target_pairs={{0,16},{1,17},{2,18},{3,19},{4,20},{5,21},{6,22},{7,23},{8,24},{9,... | collective-permute-start | bytes 442376 | tf_op jit(solution)/shard_map/ppermute | solution.py:219
  14.7 18.3 %collective-permute-start.23 = (bf16[48,1536]{1,0:T(8,128)(2,1)}, bf16[48,1536]{1,0:T(8,128)(2,1)S(1)}, u32[]{:S(2)}, u32[]{:S(2)}) collective-permute-start(bf16[48,1536]{1,0:T(8,128)(2,1)} %bitcast.288), channel_id=1, source_target_pairs={{0,24},{1,25},{2,26},{3,27},{4,28},{5,29},{6,30},{7,31},{8,16},{9,... | collective-permute-start | bytes 442376 | tf_op jit(solution)/shard_map/ppermute | solution.py:219
  18.0 16.5 %collective-permute-start.1 = (bf16[208,384]{1,0:T(8,128)(2,1)S(1)}, bf16[208,384]{1,0:T(8,128)(2,1)S(1)}, u32[]{:S(2)}, u32[]{:S(2)}) collective-permute-start(bf16[208,384]{1,0:T(8,128)(2,1)S(1)} %get-tuple-element.114), channel_id=1, source_target_pairs={{0,8},{1,9},{2,10},{3,11},{4,12},{5,13},{6,14},{7,15},{8,0},{9,1},... | collective-permute-start | bytes 479240 | tf_op jit(solution)/shard_map/ppermute | solution.py:219
  19.0 27.0 %collective-permute-start.14 = (bf16[4,48,1536]{2,1,0:T(8,128)(2,1)S(1)}, bf16[4,48,1536]{2,1,0:T(8,128)(2,1)S(1)}, u32[]{:S(2)}, u32[]{:S(2)}) collective-permute-start(bf16[4,48,1536]{2,1,0:T(8,128)(2,1)S(1)} %pad_maximum_fusion.3.refs_0_), channel_id=1, source_target_pairs={{0,4},{1,5},{2,3},{3,2},{4,0},{5,1},{6,7},{7,6},{8,12},{9,13},{10,... | collective-permute-start | bytes 1769480 | tf_op jit(solution)/shard_map/ppermute | solution.py:219
  20.5 27.2 %collective-permute-start.15 = (bf16[4,48,1536]{2,1,0:T(8,128)(2,1)S(1)}, bf16[4,48,1536]{2,1,0:T(8,128)(2,1)S(1)}, u32[]{:S(2)}, u32[]{:S(2)}) collective-permute-start(bf16[4,48,1536]{2,1,0:T(8,128)(2,1)S(1)} %pad_maximum_fusion.3.refs_0_), channel_id=1, source_target_pairs={{0,1},{1,0},{2,6},{3,7},{4,5},{5,4},{6,2},{7,3},{8,9},{9,8},{10,14... | collective-permute-start | bytes 1769480 | tf_op jit(solution)/shard_map/ppermute | solution.py:219
  30.6 13.2 %collective-permute-start.2 = (bf16[208,384]{1,0:T(8,128)(2,1)S(1)}, bf16[208,384]{1,0:T(8,128)(2,1)S(1)}, u32[]{:S(2)}, u32[]{:S(2)}) collective-permute-start(bf16[208,384]{1,0:T(8,128)(2,1)S(1)} %get-tuple-element.114), channel_id=1, source_target_pairs={{0,16},{1,17},{2,18},{3,19},{4,20},{5,21},{6,22},{7,23},{8,24},{9,... | collective-permute-start | bytes 479240 | tf_op jit(solution)/shard_map/ppermute | solution.py:219
  34.5 14.8 %collective-permute-start.17 = (bf16[4,48,1536]{2,1,0:T(8,128)(2,1)S(1)}, bf16[4,48,1536]{2,1,0:T(8,128)(2,1)S(1)}, u32[]{:S(2)}, u32[]{:S(2)}) collective-permute-start(bf16[4,48,1536]{2,1,0:T(8,128)(2,1)S(1)} %pad_maximum_fusion.3.refs_0_), channel_id=1, source_target_pairs={{0,2},{1,3},{2,0},{3,1},{4,6},{5,7},{6,4},{7,5},{8,10},{9,11},{10,... | collective-permute-start | bytes 1769480 | tf_op jit(solution)/shard_map/ppermute | solution.py:219
  43.9 52.3 %collective-permute-start = (bf16[2,256,768]{2,0,1:T(2,128)(2,1)S(1)}, bf16[2,256,768]{2,0,1:T(2,128)(2,1)S(1)}, u32[]{:S(2)}, u32[]{:S(2)}) collective-permute-start(bf16[2,256,768]{2,0,1:T(2,128)(2,1)S(1)} %get-tuple-element.97), channel_id=1, source_target_pairs={{0,1},{1,0},{2,3},{3,2},{4,5},{5,4},{6,7},{7,6},{8,9},{9,8},{10,11... | collective-permute-start | bytes 2359304 | tf_op jit(solution)/shard_map/ppermute | solution.py:380
  45.6 51.2 %collective-permute-start.32 = (bf16[2,256,768]{2,1,0:T(8,128)(2,1)S(1)}, bf16[2,256,768]{2,1,0:T(8,128)(2,1)}, u32[]{:S(2)}, u32[]{:S(2)}) collective-permute-start(bf16[2,256,768]{2,1,0:T(8,128)(2,1)S(1)} %bitcast.277), channel_id=1, source_target_pairs={{0,1},{1,0},{2,3},{3,2},{4,5},{5,4},{6,7},{7,6},{8,9},{9,8},{10,11... | collective-permute-start | bytes 2359304 | tf_op jit(solution)/shard_map/ppermute | solution.py:380
  46.0 15.9 %collective-permute-start.24 = (bf16[4,48,1536]{2,1,0:T(8,128)(2,1)S(1)}, bf16[4,48,1536]{2,1,0:T(8,128)(2,1)S(1)}, u32[]{:S(2)}, u32[]{:S(2)}) collective-permute-start(bf16[4,48,1536]{2,1,0:T(8,128)(2,1)S(1)} %pad_maximum_fusion.4.refs_0_), channel_id=1, source_target_pairs={{0,4},{1,5},{2,3},{3,2},{4,0},{5,1},{6,7},{7,6},{8,12},{9,13},{10,... | collective-permute-start | bytes 1769480 | tf_op jit(solution)/shard_map/ppermute | solution.py:219
  47.8 45.6 %collective-permute-start.25 = (bf16[4,48,1536]{2,1,0:T(8,128)(2,1)S(1)}, bf16[4,48,1536]{2,1,0:T(8,128)(2,1)S(1)}, u32[]{:S(2)}, u32[]{:S(2)}) collective-permute-start(bf16[4,48,1536]{2,1,0:T(8,128)(2,1)S(1)} %pad_maximum_fusion.4.refs_0_), channel_id=1, source_target_pairs={{0,1},{1,0},{2,6},{3,7},{4,5},{5,4},{6,2},{7,3},{8,9},{9,8},{10,14... | collective-permute-start | bytes 1769480 | tf_op jit(solution)/shard_map/ppermute | solution.py:219
  49.3 45.7 %collective-permute-start.27 = (bf16[4,48,1536]{2,1,0:T(8,128)(2,1)S(1)}, bf16[4,48,1536]{2,1,0:T(8,128)(2,1)S(1)}, u32[]{:S(2)}, u32[]{:S(2)}) collective-permute-start(bf16[4,48,1536]{2,1,0:T(8,128)(2,1)S(1)} %pad_maximum_fusion.4.refs_0_), channel_id=1, source_target_pairs={{0,2},{1,3},{2,0},{3,1},{4,6},{5,7},{6,4},{7,5},{8,10},{9,11},{10,... | collective-permute-start | bytes 1769480 | tf_op jit(solution)/shard_map/ppermute | solution.py:219
  61.9 34.9 %collective-permute-start.4 = (bf16[4,208,384]{2,1,0:T(8,128)(2,1)S(1)}, bf16[4,208,384]{2,1,0:T(8,128)(2,1)S(1)}, u32[]{:S(2)}, u32[]{:S(2)}) collective-permute-start(bf16[4,208,384]{2,1,0:T(8,128)(2,1)S(1)} %pad_maximum_fusion.2.refs_0_), channel_id=1, source_target_pairs={{0,4},{1,5},{2,3},{3,2},{4,0},{5,1},{6,7},{7,6},{8,12},{9,13},{10,... | collective-permute-start | bytes 1916936 | tf_op jit(solution)/shard_map/ppermute | solution.py:219
  93.3 16.0 %collective-permute-start.5 = (bf16[4,208,384]{2,1,0:T(8,128)(2,1)S(1)}, bf16[4,208,384]{2,1,0:T(8,128)(2,1)S(1)}, u32[]{:S(2)}, u32[]{:S(2)}) collective-permute-start(bf16[4,208,384]{2,1,0:T(8,128)(2,1)S(1)} %pad_maximum_fusion.2.refs_0_), channel_id=1, source_target_pairs={{0,1},{1,0},{2,6},{3,7},{4,5},{5,4},{6,2},{7,3},{8,9},{9,8},{10,14... | collective-permute-start | bytes 1916936 | tf_op jit(solution)/shard_map/ppermute | solution.py:219
  95.9 19.8 %collective-permute-start.16 = (bf16[4,48,1536]{2,1,0:T(8,128)(2,1)}, bf16[4,48,1536]{2,1,0:T(8,128)(2,1)S(1)}, u32[]{:S(2)}, u32[]{:S(2)}) collective-permute-start(bf16[4,48,1536]{2,1,0:T(8,128)(2,1)} %copy-done.4), channel_id=1, source_target_pairs={{0,1},{1,0},{2,6},{3,7},{4,5},{5,4},{6,2},{7,3},{8,9},{9,8},{10,14... | collective-permute-start | bytes 1769480 | tf_op jit(solution)/shard_map/ppermute | solution.py:219
  96.2 20.3 %collective-permute-start.18 = (bf16[4,48,1536]{2,1,0:T(8,128)(2,1)}, bf16[4,48,1536]{2,1,0:T(8,128)(2,1)S(1)}, u32[]{:S(2)}, u32[]{:S(2)}) collective-permute-start(bf16[4,48,1536]{2,1,0:T(8,128)(2,1)} %copy-done.4), channel_id=1, source_target_pairs={{0,2},{1,3},{2,0},{3,1},{4,6},{5,7},{6,4},{7,5},{8,10},{9,11},{10,... | collective-permute-start | bytes 1769480 | tf_op jit(solution)/shard_map/ppermute | solution.py:219
  96.8 21.9 %collective-permute-start.19 = (bf16[4,48,1536]{2,1,0:T(8,128)(2,1)}, bf16[4,48,1536]{2,1,0:T(8,128)(2,1)S(1)}, u32[]{:S(2)}, u32[]{:S(2)}) collective-permute-start(bf16[4,48,1536]{2,1,0:T(8,128)(2,1)} %copy-done.6), channel_id=1, source_target_pairs={{0,2},{1,3},{2,0},{3,1},{4,6},{5,7},{6,4},{7,5},{8,10},{9,11},{10,... | collective-permute-start | bytes 1769480 | tf_op jit(solution)/shard_map/ppermute | solution.py:219
  96.9 34.2 %collective-permute-start.6 = (bf16[4,208,384]{2,1,0:T(8,128)(2,1)S(1)}, bf16[4,208,384]{2,1,0:T(8,128)(2,1)}, u32[]{:S(2)}, u32[]{:S(2)}) collective-permute-start(bf16[4,208,384]{2,1,0:T(8,128)(2,1)S(1)} %collective-permute-done.4.refs_1_), channel_id=1, source_target_pairs={{0,1},{1,0},{2,6},{3,7},{4,5},{5,4},{6,2},{7,3},{8,9},{9,8},{10,14... | collective-permute-start | bytes 1916936 | tf_op jit(solution)/shard_map/ppermute | solution.py:219
  109.3 19.6 %collective-permute-start.26 = (bf16[4,48,1536]{2,1,0:T(8,128)(2,1)S(1)}, bf16[4,48,1536]{2,1,0:T(8,128)(2,1)}, u32[]{:S(2)}, u32[]{:S(2)}) collective-permute-start(bf16[4,48,1536]{2,1,0:T(8,128)(2,1)S(1)} %collective-permute-done.24.refs_1_), channel_id=1, source_target_pairs={{0,1},{1,0},{2,6},{3,7},{4,5},{5,4},{6,2},{7,3},{8,9},{9,8},{10,14... | collective-permute-start | bytes 1769480 | tf_op jit(solution)/shard_map/ppermute | solution.py:219
  115.7 13.3 %collective-permute-start.28 = (bf16[4,48,1536]{2,1,0:T(8,128)(2,1)S(1)}, bf16[4,48,1536]{2,1,0:T(8,128)(2,1)S(1)}, u32[]{:S(2)}, u32[]{:S(2)}) collective-permute-start(bf16[4,48,1536]{2,1,0:T(8,128)(2,1)S(1)} %collective-permute-done.24.refs_1_), channel_id=1, source_target_pairs={{0,2},{1,3},{2,0},{3,1},{4,6},{5,7},{6,4},{7,5},{8,10},{9,11},{10,... | collective-permute-start | bytes 1769480 | tf_op jit(solution)/shard_map/ppermute | solution.py:219
  128.9 28.2 %collective-permute-start.7 = (bf16[4,208,384]{2,1,0:T(8,128)(2,1)S(1)}, bf16[4,208,384]{2,1,0:T(8,128)(2,1)}, u32[]{:S(2)}, u32[]{:S(2)}) collective-permute-start(bf16[4,208,384]{2,1,0:T(8,128)(2,1)S(1)} %pad_maximum_fusion.2.refs_0_), channel_id=1, source_target_pairs={{0,2},{1,3},{2,0},{3,1},{4,6},{5,7},{6,4},{7,5},{8,10},{9,11},{10,... | collective-permute-start | bytes 1916936 | tf_op jit(solution)/shard_map/ppermute | solution.py:219
  129.7 27.4 %collective-permute-start.8 = (bf16[4,208,384]{2,1,0:T(8,128)(2,1)S(1)}, bf16[4,208,384]{2,1,0:T(8,128)(2,1)}, u32[]{:S(2)}, u32[]{:S(2)}) collective-permute-start(bf16[4,208,384]{2,1,0:T(8,128)(2,1)S(1)} %collective-permute-done.4.refs_1_), channel_id=1, source_target_pairs={{0,2},{1,3},{2,0},{3,1},{4,6},{5,7},{6,4},{7,5},{8,10},{9,11},{10,... | collective-permute-start | bytes 1916936 | tf_op jit(solution)/shard_map/ppermute | solution.py:219
  131.1 26.0 %collective-permute-start.9 = (bf16[4,208,384]{2,1,0:T(8,128)(2,1)S(1)}, bf16[4,208,384]{2,1,0:T(8,128)(2,1)}, u32[]{:S(2)}, u32[]{:S(2)}) collective-permute-start(bf16[4,208,384]{2,1,0:T(8,128)(2,1)S(1)} %collective-permute-done.5.refs_2_), channel_id=1, source_target_pairs={{0,2},{1,3},{2,0},{3,1},{4,6},{5,7},{6,4},{7,5},{8,10},{9,11},{10,... | collective-permute-start | bytes 1916936 | tf_op jit(solution)/shard_map/ppermute | solution.py:219
  131.1 26.0 %collective-permute-start.10 = (bf16[4,208,384]{2,1,0:T(8,128)(2,1)}, bf16[4,208,384]{2,1,0:T(8,128)(2,1)}, u32[]{:S(2)}, u32[]{:S(2)}) collective-permute-start(bf16[4,208,384]{2,1,0:T(8,128)(2,1)} %collective-permute-done.6.refs_3_), channel_id=1, source_target_pairs={{0,2},{1,3},{2,0},{3,1},{4,6},{5,7},{6,4},{7,5},{8,10},{9,11},{10,... | collective-permute-start | bytes 1916936 | tf_op jit(solution)/shard_map/ppermute | solution.py:219
  132.5 20.4 %collective-permute-start.30 = (bf16[4,48,1536]{2,1,0:T(8,128)(2,1)}, bf16[4,48,1536]{2,1,0:T(8,128)(2,1)}, u32[]{:S(2)}, u32[]{:S(2)}) collective-permute-start(bf16[4,48,1536]{2,1,0:T(8,128)(2,1)} %collective-permute-done.26.refs_3_), channel_id=1, source_target_pairs={{0,2},{1,3},{2,0},{3,1},{4,6},{5,7},{6,4},{7,5},{8,10},{9,11},{10,... | collective-permute-start | bytes 1769480 | tf_op jit(solution)/shard_map/ppermute | solution.py:219
  316.6 85.0 %collective-permute-start.55 = (bf16[4,4,48,1536]{3,2,1,0:T(8,128)(2,1)}, bf16[4,4,48,1536]{3,2,1,0:T(8,128)(2,1)}, u32[]{:S(2)}, u32[]{:S(2)}) collective-permute-start(bf16[4,4,48,1536]{3,2,1,0:T(8,128)(2,1)} %get-tuple-element.45), channel_id=1, source_target_pairs={{0,2},{1,3},{2,0},{3,1},{4,6},{5,7},{6,4},{7,5},{8,10},{9,11},{10,... | collective-permute-start | bytes 7077896 | tf_op jit(solution)/shard_map/ppermute | solution.py:219
  320.9 85.5 %collective-permute-start.48 = (bf16[4,4,48,1536]{3,2,1,0:T(8,128)(2,1)}, bf16[4,4,48,1536]{3,2,1,0:T(8,128)(2,1)}, u32[]{:S(2)}, u32[]{:S(2)}) collective-permute-start(bf16[4,4,48,1536]{3,2,1,0:T(8,128)(2,1)} %get-tuple-element.43), channel_id=1, source_target_pairs={{0,2},{1,3},{2,0},{3,1},{4,6},{5,7},{6,4},{7,5},{8,10},{9,11},{10,... | collective-permute-start | bytes 7077896 | tf_op jit(solution)/shard_map/ppermute | solution.py:219
  321.4 22.6 %collective-permute-start.41 = (bf16[4,4,48,384]{3,2,1,0:T(8,128)(2,1)S(1)}, bf16[4,4,48,384]{3,2,1,0:T(8,128)(2,1)}, u32[]{:S(2)}, u32[]{:S(2)}) collective-permute-start(bf16[4,4,48,384]{3,2,1,0:T(8,128)(2,1)S(1)} %get-tuple-element.41), channel_id=1, source_target_pairs={{0,2},{1,3},{2,0},{3,1},{4,6},{5,7},{6,4},{7,5},{8,10},{9,11},{10,... | collective-permute-start | bytes 1769480 | tf_op jit(solution)/shard_map/ppermute | solution.py:219
  333.8 27.9 %collective-permute-start.31 = (bf16[2,256,768]{2,0,1:T(2,128)(2,1)}, bf16[2,256,768]{2,0,1:T(2,128)(2,1)}, u32[]{:S(2)}, u32[]{:S(2)}) collective-permute-start(bf16[2,256,768]{2,0,1:T(2,128)(2,1)} %bitcast.261), channel_id=1, source_target_pairs={{0,1},{1,0},{2,3},{3,2},{4,5},{5,4},{6,7},{7,6},{8,9},{9,8},{10,11... | collective-permute-start | bytes 2359304 | tf_op jit(solution)/shard_map/ppermute | solution.py:380
  347.0 13.8 %collective-permute-start.43 = (bf16[4,48,384]{2,1,0:T(8,128)(2,1)}, bf16[4,48,384]{2,1,0:T(8,128)(2,1)}, u32[]{:S(2)}, u32[]{:S(2)}) collective-permute-start(bf16[4,48,384]{2,1,0:T(8,128)(2,1)} %get-tuple-element.107), channel_id=1, source_target_pairs={{0,1},{1,0},{2,6},{3,7},{4,5},{5,4},{6,2},{7,3},{8,9},{9,8},{10,14... | collective-permute-start | bytes 442376 | tf_op jit(solution)/shard_map/ppermute | solution.py:219
  355.8 20.2 %collective-permute-start.33 = (bf16[2,256,768]{2,0,1:T(2,128)(2,1)S(1)}, bf16[2,256,768]{2,0,1:T(2,128)(2,1)S(1)}, u32[]{:S(2)}, u32[]{:S(2)}) collective-permute-start(bf16[2,256,768]{2,0,1:T(2,128)(2,1)S(1)} %bitcast.278), channel_id=1, source_target_pairs={{0,1},{1,0},{2,3},{3,2},{4,5},{5,4},{6,7},{7,6},{8,9},{9,8},{10,11... | collective-permute-start | bytes 2359304 | tf_op jit(solution)/shard_map/ppermute | solution.py:380
  360.7 38.0 %collective-permute-start.34 = (bf16[4,4,160,384]{3,2,1,0:T(8,128)(2,1)S(1)}, bf16[4,4,160,384]{3,2,1,0:T(8,128)(2,1)S(1)}, u32[]{:S(2)}, u32[]{:S(2)}) collective-permute-start(bf16[4,4,160,384]{3,2,1,0:T(8,128)(2,1)S(1)} %get-tuple-element.39), channel_id=1, source_target_pairs={{0,2},{1,3},{2,0},{3,1},{4,6},{5,7},{6,4},{7,5},{8,10},{9,11},{10,... | collective-permute-start | bytes 5898248 | tf_op jit(solution)/shard_map/ppermute | solution.py:219
  361.8 16.6 %collective-permute-start.42 = (bf16[4,48,384]{2,1,0:T(8,128)(2,1)S(1)}, bf16[4,48,384]{2,1,0:T(8,128)(2,1)S(1)}, u32[]{:S(2)}, u32[]{:S(2)}) collective-permute-start(bf16[4,48,384]{2,1,0:T(8,128)(2,1)S(1)} %copy-done.42), channel_id=1, source_target_pairs={{0,1},{1,0},{2,6},{3,7},{4,5},{5,4},{6,2},{7,3},{8,9},{9,8},{10,14... | collective-permute-start | bytes 442376 | tf_op jit(solution)/shard_map/ppermute | solution.py:219
  400.1 18.8 %collective-permute-start.35 = (bf16[4,160,384]{2,1,0:T(8,128)(2,1)S(1)}, bf16[4,160,384]{2,1,0:T(8,128)(2,1)S(1)}, u32[]{:S(2)}, u32[]{:S(2)}) collective-permute-start(bf16[4,160,384]{2,1,0:T(8,128)(2,1)S(1)} %get-tuple-element.85), channel_id=1, source_target_pairs={{0,1},{1,0},{2,6},{3,7},{4,5},{5,4},{6,2},{7,3},{8,9},{9,8},{10,14... | collective-permute-start | bytes 1474568 | tf_op jit(solution)/shard_map/ppermute | solution.py:219
  404.3 22.3 %collective-permute-start.57 = (bf16[4,48,1536]{2,1,0:T(8,128)(2,1)S(1)}, bf16[4,48,1536]{2,1,0:T(8,128)(2,1)S(1)}, u32[]{:S(2)}, u32[]{:S(2)}) collective-permute-start(bf16[4,48,1536]{2,1,0:T(8,128)(2,1)S(1)} %get-tuple-element.80), channel_id=1, source_target_pairs={{0,1},{1,0},{2,6},{3,7},{4,5},{5,4},{6,2},{7,3},{8,9},{9,8},{10,14... | collective-permute-start | bytes 1769480 | tf_op jit(solution)/shard_map/ppermute | solution.py:219
  404.9 39.7 %collective-permute-start.56 = (bf16[4,48,1536]{2,1,0:T(8,128)(2,1)S(1)}, bf16[4,48,1536]{2,1,0:T(8,128)(2,1)S(1)}, u32[]{:S(2)}, u32[]{:S(2)}) collective-permute-start(bf16[4,48,1536]{2,1,0:T(8,128)(2,1)S(1)} %get-tuple-element.79), channel_id=1, source_target_pairs={{0,1},{1,0},{2,6},{3,7},{4,5},{5,4},{6,2},{7,3},{8,9},{9,8},{10,14... | collective-permute-start | bytes 1769480 | tf_op jit(solution)/shard_map/ppermute | solution.py:219
  409.2 14.2 %collective-permute-start.37 = (bf16[4,160,384]{2,1,0:T(8,128)(2,1)S(1)}, bf16[4,160,384]{2,1,0:T(8,128)(2,1)S(1)}, u32[]{:S(2)}, u32[]{:S(2)}) collective-permute-start(bf16[4,160,384]{2,1,0:T(8,128)(2,1)S(1)} %fusion.17), channel_id=1, source_target_pairs={{0,4},{1,5},{2,3},{3,2},{4,0},{5,1},{6,7},{7,6},{8,12},{9,13},{10,... | collective-permute-start | bytes 1474568 | tf_op jit(solution)/shard_map/ppermute | solution.py:219
  409.9 28.3 %collective-permute-start.50 = (bf16[4,48,1536]{2,1,0:T(8,128)(2,1)S(1)}, bf16[4,48,1536]{2,1,0:T(8,128)(2,1)S(1)}, u32[]{:S(2)}, u32[]{:S(2)}) collective-permute-start(bf16[4,48,1536]{2,1,0:T(8,128)(2,1)S(1)} %get-tuple-element.82), channel_id=1, source_target_pairs={{0,1},{1,0},{2,6},{3,7},{4,5},{5,4},{6,2},{7,3},{8,9},{9,8},{10,14... | collective-permute-start | bytes 1769480 | tf_op jit(solution)/shard_map/ppermute | solution.py:219
  423.6 15.5 %collective-permute-start.38 = (bf16[160,384]{1,0:T(8,128)(2,1)S(1)}, bf16[160,384]{1,0:T(8,128)(2,1)S(1)}, u32[]{:S(2)}, u32[]{:S(2)}) collective-permute-start(bf16[160,384]{1,0:T(8,128)(2,1)S(1)} %get-tuple-element.108), channel_id=1, source_target_pairs={{0,8},{1,9},{2,10},{3,11},{4,12},{5,13},{6,14},{7,15},{8,0},{9,1},... | collective-permute-start | bytes 368648 | tf_op jit(solution)/shard_map/ppermute | solution.py:219
  424.2 15.7 %collective-permute-start.39 = (bf16[160,384]{1,0:T(8,128)(2,1)S(1)}, bf16[160,384]{1,0:T(8,128)(2,1)S(1)}, u32[]{:S(2)}, u32[]{:S(2)}) collective-permute-start(bf16[160,384]{1,0:T(8,128)(2,1)S(1)} %get-tuple-element.110), channel_id=1, source_target_pairs={{0,16},{1,17},{2,18},{3,19},{4,20},{5,21},{6,22},{7,23},{8,24},{9,... | collective-permute-start | bytes 368648 | tf_op jit(solution)/shard_map/ppermute | solution.py:219
  426.7 14.5 %collective-permute-start.40 = (bf16[160,384]{1,0:T(8,128)(2,1)S(1)}, bf16[160,384]{1,0:T(8,128)(2,1)S(1)}, u32[]{:S(2)}, u32[]{:S(2)}) collective-permute-start(bf16[160,384]{1,0:T(8,128)(2,1)S(1)} %get-tuple-element.109), channel_id=1, source_target_pairs={{0,24},{1,25},{2,26},{3,27},{4,28},{5,29},{6,30},{7,31},{8,16},{9,... | collective-permute-start | bytes 368648 | tf_op jit(solution)/shard_map/ppermute | solution.py:219
  439.1 17.3 %collective-permute-start.49 = (bf16[4,48,1536]{2,1,0:T(8,128)(2,1)S(1)}, bf16[4,48,1536]{2,1,0:T(8,128)(2,1)S(1)}, u32[]{:S(2)}, u32[]{:S(2)}) collective-permute-start(bf16[4,48,1536]{2,1,0:T(8,128)(2,1)S(1)} %get-tuple-element.81), channel_id=1, source_target_pairs={{0,1},{1,0},{2,6},{3,7},{4,5},{5,4},{6,2},{7,3},{8,9},{9,8},{10,14... | collective-permute-start | bytes 1769480 | tf_op jit(solution)/shard_map/ppermute | solution.py:219
  439.9 16.7 %collective-permute-start.51 = (bf16[4,48,1536]{2,1,0:T(8,128)(2,1)S(1)}, bf16[4,48,1536]{2,1,0:T(8,128)(2,1)}, u32[]{:S(2)}, u32[]{:S(2)}) collective-permute-start(bf16[4,48,1536]{2,1,0:T(8,128)(2,1)S(1)} %fusion.13), channel_id=1, source_target_pairs={{0,4},{1,5},{2,3},{3,2},{4,0},{5,1},{6,7},{7,6},{8,12},{9,13},{10,... | collective-permute-start | bytes 1769480 | tf_op jit(solution)/shard_map/ppermute | solution.py:219
  459.2 16.1 %collective-permute-start.53 = (bf16[48,1536]{1,0:T(8,128)(2,1)S(1)}, bf16[48,1536]{1,0:T(8,128)(2,1)S(1)}, u32[]{:S(2)}, u32[]{:S(2)}) collective-permute-start(bf16[48,1536]{1,0:T(8,128)(2,1)S(1)} %get-tuple-element.105), channel_id=1, source_target_pairs={{0,16},{1,17},{2,18},{3,19},{4,20},{5,21},{6,22},{7,23},{8,24},{9,... | collective-permute-start | bytes 442376 | tf_op jit(solution)/shard_map/ppermute | solution.py:219
  461.5 13.8 %collective-permute-start.54 = (bf16[48,1536]{1,0:T(8,128)(2,1)S(1)}, bf16[48,1536]{1,0:T(8,128)(2,1)S(1)}, u32[]{:S(2)}, u32[]{:S(2)}) collective-permute-start(bf16[48,1536]{1,0:T(8,128)(2,1)S(1)} %get-tuple-element.104), channel_id=1, source_target_pairs={{0,24},{1,25},{2,26},{3,27},{4,28},{5,29},{6,30},{7,31},{8,16},{9,... | collective-permute-start | bytes 442376 | tf_op jit(solution)/shard_map/ppermute | solution.py:219
  (73 other events, 785.8 us)
